TPU v7x, 512 devices: a whole 4x4x16 slice. The times are simulated.
512 devices in a mesh: section: 32 (over y, z_lo), row: 4 (over z_hi, core), col: 4 (over x).
Axes of the slice: x: 4, y: 4, z: 16 (z_hi: 2, z_lo: 8; z = z_hi * 8 + z_lo), core: 2. Of those that a mesh axis runs over, the one named last changes fastest.
Arguments:
- inputs: bfloat16 [512, 6144], P('row', 'col'), may hold values from -6 to 6
- cotangent: bfloat16 [512, 6144], P('row', 'col'), may hold values from -3 to 3
- ln_gain: float32 [6144], P('col'), may hold values from 0.1 to 1.9
- ln_bias: float32 [6144], P('col'), may hold values from -3 to 3
- w_in: bfloat16 [6144, 24576], P('row', ('section', 'col')), may hold values from -0.078125 to 0.078125
- w_out: bfloat16 [24576, 6144], P(('section', 'row'), 'col'), may hold values from -0.0390625 to 0.0390625
Outputs:
- outputs: bfloat16 [512, 6144], P('row', 'col')
- grad_x: bfloat16 [512, 6144], P('row', 'col')
- grad_in: bfloat16 [6144, 24576], P('row', ('section', 'col'))
- grad_out: bfloat16 [24576, 6144], P(('section', 'row'), 'col')
All inputs are finite; a program needn't handle non-finite values.
Results may differ from a plain program's by a relative error of at most 0.0062.
Values may be sent and summed in bfloat16 or wider, within the bound.
A program may use at most 64 MiB of HBM per device.

v0:
```python
import jax
import jax.numpy as jnp
from jax import lax
from jax.sharding import PartitionSpec as P

EPS = 1e-05
SLOPE = 0.7978845608028654
CUBIC = 0.044715


def gelu(values):
    return 0.5 * values * (1.0 + jnp.tanh(SLOPE * (values + CUBIC * values * values * values)))


def gelu_slope(values):
    inner = jnp.tanh(SLOPE * (values + CUBIC * values * values * values))
    return 0.5 * (1.0 + inner) + 0.5 * values * (1.0 - inner * inner) * SLOPE * (
        1.0 + 3.0 * CUBIC * values * values
    )


def per_device(inputs, cotangent, ln_gain, ln_bias, w_in, w_out):
    row_count, feature_cols = inputs.shape
    model_width = feature_cols * lax.axis_size("col")
    in_panel, out_panel = (
        lax.all_gather(w_in, "row", axis=0, tiled=True),
        lax.all_gather(w_out, "row", axis=0, tiled=True),
    )
    stream_f32 = inputs.astype(jnp.float32)
    first_sum, square_sum = lax.psum(
        (
            jnp.sum(stream_f32, -1, keepdims=True),
            jnp.sum(stream_f32 * stream_f32, -1, keepdims=True),
        ),
        "col",
    )
    row_mean = first_sum / model_width
    inv_scale = lax.rsqrt(square_sum / model_width - row_mean * row_mean + EPS)
    scaled = (stream_f32 - row_mean) * inv_scale
    normed = lax.all_gather(
        (scaled * ln_gain + ln_bias).astype(jnp.bfloat16), "col", axis=1, tiled=True
    )
    hidden = jnp.dot(normed, in_panel, preferred_element_type=jnp.float32)
    active_row = lax.all_gather(gelu(hidden).astype(jnp.bfloat16), "col", axis=1, tiled=True)
    branch_part = jnp.dot(active_row, out_panel, preferred_element_type=jnp.float32)
    branch_total = lax.psum(branch_part, "section")
    outputs = (stream_f32 + branch_total).astype(jnp.bfloat16)
    panel_rows = out_panel
    grad_act = lax.psum_scatter(
        lax.dot_general(
            panel_rows, cotangent, (((1,), (1,)), ((), ())), preferred_element_type=jnp.float32
        ),
        "col",
        scatter_dimension=0,
        tiled=True,
    ).T
    grad_hid = (grad_act * gelu_slope(hidden)).astype(jnp.bfloat16)
    panel_rows = in_panel
    slab_norm = lax.psum_scatter(
        lax.dot_general(
            panel_rows, grad_hid, (((1,), (1,)), ((), ())), preferred_element_type=jnp.float32
        ),
        "col",
        scatter_dimension=0,
        tiled=True,
    ).T
    grad_norm = lax.psum(slab_norm, "section")
    grad_scaled = grad_norm * ln_gain
    first_total, second_total = lax.psum(
        (jnp.sum(grad_scaled, -1, keepdims=True), jnp.sum(grad_scaled * scaled, -1, keepdims=True)),
        "col",
    )
    delta = inv_scale * (
        grad_scaled - first_total / model_width - scaled * (second_total / model_width)
    )
    grad_x = (cotangent.astype(jnp.float32) + delta).astype(jnp.bfloat16)
    owned_norm, owned_act = (
        lax.all_to_all(normed, "row", split_axis=1, concat_axis=0, tiled=True),
        lax.all_to_all(active_row, "row", split_axis=1, concat_axis=0, tiled=True),
    )
    grad_rows = lax.all_gather(cotangent, "row", axis=0, tiled=True)
    hid_rows = lax.all_gather(grad_hid, "row", axis=0, tiled=True)
    step_in = lax.dot_general(
        owned_norm, hid_rows, (((0,), (0,)), ((), ())), preferred_element_type=jnp.float32
    )
    step_out = lax.dot_general(
        owned_act, grad_rows, (((0,), (0,)), ((), ())), preferred_element_type=jnp.float32
    )
    return (outputs, grad_x, step_in.astype(jnp.bfloat16), step_out.astype(jnp.bfloat16))


def solution(mesh):
    return jax.shard_map(
        per_device,
        mesh=mesh,
        in_specs=(
            P("row", "col"),
            P("row", "col"),
            P("col"),
            P("col"),
            P("row", ("section", "col")),
            P(("section", "row"), "col"),
        ),
        out_specs=(
            P("row", "col"),
            P("row", "col"),
            P("row", ("section", "col")),
            P(("section", "row"), "col"),
        ),
        check_vma=False,
    )
```

profile of v0, /device:TPU:6, one launch (start us, length us, event | category | flops | bytes accessed | tf_op | source)
XLA Modules:
  0.0 875.4 jit_solution(3544762760448441258)
XLA Ops:
  8.0 1.2 convert_reduce_fusion
  9.1 12.4 %all-reduce.2 = (f32[128,1]{0,1:T(1,128)S(1)}, f32[128,1]{0,1:T(1,128)S(1)}) all-reduce(f32[128,1]{0,1:T(1,128)S(1)} %bitcast.48, f32[128,1]{0,1:T(1,128)S(1)} %bitcast.47), channel_id=1, replica_groups=mesh['section'=32,'row'=4,'col'=4] {'col'}, use_global_device_ids=true, to_apply=%region_3.0 | all-reduce | flops 256 | bytes 2048 | tf_op jit(solution)/shard_map/psum | solution.py:30
  21.5 2.1 fusion.5
  24.4 71.6 %all-gather.9.cloned.1.call-done = bf16[768,1536]{1,0:T(8,128)(2,1)} async-done(((bf16[192,1536]{1,0:T(8,128)(2,1)}), bf16[768,1536]{1,0:T(8,128)(2,1)}) %all-gather.9.cloned.1.call-update) | async-done | bytes 2359312 | tf_op jit(solution)/shard_map/all_gather | solution.py:27
  96.0 3.2 fusion.23
  99.2 24.8 %all-gather.5.cloned.1.call-done = bf16[128,6144]{1,0:T(8,128)(2,1)} async-done(((bf16[128,1536]{1,0:T(8,128)(2,1)}), bf16[128,6144]{1,0:T(8,128)(2,1)}) %all-gather.5.cloned.1.call-update) | async-done | bytes 1572880 | tf_op jit(solution)/shard_map/all_gather | solution.py:40
  124.1 84.8 %all-gather.7.cloned.1.call-done = bf16[6144,192]{0,1:T(8,128)(2,1)} async-done(((bf16[1536,192]{0,1:T(8,128)(2,1)}), bf16[6144,192]{0,1:T(8,128)(2,1)}) %all-gather.7.cloned.1.call-update) | async-done | bytes 2359312 | tf_op jit(solution)/shard_map/all_gather | solution.py:26
  208.9 22.9 %reduce-scatter.3.cloned.1.call-done = f32[192,128]{1,0:T(8,128)} async-done(((f32[768,128]{1,0:T(8,128)}), f32[192,128]{1,0:T(8,128)}) %reduce-scatter.3.cloned.1.call-update) | async-done | bytes 98320 | tf_op jit(solution)/shard_map/reduce_scatter | solution.py:49
  231.8 2.9 fusion.21
  234.7 2.2 convolution_bitcast_fusion
  237.0 13.0 %all_gather.20 = bf16[128,768]{0,1:T(8,128)(2,1)} all-gather(bf16[128,192]{0,1:T(8,128)(2,1)S(1)} %get-tuple-element.17), channel_id=1, replica_groups=mesh['section'=32,'row'=4,'col'=4] {'col'}, dimensions={1}, use_global_device_ids=true | all-gather | bytes 245760 | tf_op jit(solution)/shard_map/all_gather | solution.py:44
  250.0 11.5 %all-to-all-start.1 = ((bf16[128,4,192]{0,2,1:T(8,128)(2,1)}), bf16[128,4,192]{0,2,1:T(8,128)(2,1)S(1)}, u32[]{:S(2)}, u32[]{:S(2)}) async-start(bf16[128,4,192]{0,2,1:T(8,128)(2,1)} %bitcast.13), calls=%async_computation.3 | async-start | bytes 393216 | tf_op jit(solution)/shard_map/all_to_all | solution.py:79
  261.5 1.4 copy.21
  262.9 12.8 %all-to-all-done.1 = bf16[128,4,192]{0,2,1:T(8,128)(2,1)S(1)} async-done(((bf16[128,4,192]{0,2,1:T(8,128)(2,1)}), bf16[128,4,192]{0,2,1:T(8,128)(2,1)S(1)}, u32[]{:S(2)}, u32[]{:S(2)}) %all-to-all-start.1) | async-done | bytes 196640 | tf_op jit(solution)/shard_map/all_to_all | solution.py:79
  275.6 4.3 all-to-all-start
  280.6 2.3 fusion.22
  283.0 43.3 %all_gather.22 = bf16[512,192]{0,1:T(8,128)(2,1)S(1)} all-gather(bf16[128,192]{0,1:T(8,128)(2,1)S(1)} %get-tuple-element.16), channel_id=1, replica_groups=mesh['section'=32,'row'=4,'col'=4] {'row'}, dimensions={0}, use_global_device_ids=true | all-gather | bytes 245760 | tf_op jit(solution)/shard_map/all_gather | solution.py:82
  326.3 12.4 %all-gather.11.cloned.1.call-done = bf16[512,1536]{1,0:T(8,128)(2,1)} async-done(((bf16[128,1536]{1,0:T(8,128)(2,1)}), bf16[512,1536]{1,0:T(8,128)(2,1)}) %all-gather.11.cloned.1.call-update) | async-done | bytes 1572880 | tf_op jit(solution)/shard_map/all_gather | solution.py:81
  338.7 2.7 convolution_convert_fusion.1
  341.4 2.8 convolution_convert_fusion
  344.2 512.8 %all-reduce.5.cloned.1.call-done = (f32[128,1536]{1,0:T(8,128)}, f32[128,1536]{1,0:T(8,128)}) async-done(((f32[128,1536]{1,0:T(8,128)}, f32[128,1536]{1,0:T(8,128)}), (f32[128,1536]{1,0:T(8,128)}, f32[128,1536]{1,0:T(8,128)})) %all-reduce.5.cloned.1.call-update) | async-done | bytes 1572880 | tf_op jit(solution)/shard_map/psum | solution.py:46
  857.0 1.4 multiply_reduce_fusion
  858.4 7.5 all-reduce.1
  865.9 2.7 fusion.10
  (32 shorter events, 2.3 us)
Async XLA Ops:
  7.2 88.8 %copy-start.4 = (bf16[128,1536]{1,0:T(8,128)(2,1)S(1)}, bf16[128,1536]{1,0:T(8,128)(2,1)}, u32[]{:S(2)}) copy-start(bf16[128,1536]{1,0:T(8,128)(2,1)} %param.7) | copy-start | bytes 1179652
  7.2 88.8 %all-gather.9.cloned.1.call-start = ((), (), s32[]{:S(2)}) async-start(), calls=%async_computation.6 | async-start | bytes 2949120 | tf_op jit(solution)/shard_map/all_gather | solution.py:27
  7.9 116.2 %all-gather.5.cloned.1.call-start = ((), (), s32[]{:S(2)}) async-start(), calls=%async_computation.4 | async-start | bytes 1966080 | tf_op jit(solution)/shard_map/all_gather | solution.py:40
  23.6 185.3 %all-gather.7.cloned.1.call-start = ((), (), s32[]{:S(2)}) async-start(), calls=%async_computation.5 | async-start | bytes 2949120 | tf_op jit(solution)/shard_map/all_gather | solution.py:26
  24.4 207.4 %reduce-scatter.3.cloned.1.call-start = ((), (), s32[]{:S(2)}) async-start(), calls=%async_computation.7 | async-start | bytes 491520 | tf_op jit(solution)/shard_map/reduce_scatter | solution.py:49
  99.2 183.8 %reduce-scatter.5.cloned.1.call-start = ((), (), s32[]{:S(2)}) async-start(), calls=%async_computation.8 | async-start | bytes 3932160 | tf_op jit(solution)/shard_map/reduce_scatter | solution.py:59
  208.9 25.8 %copy-start.1 = (bf16[6144,192]{0,1:T(8,128)(2,1)S(1)}, bf16[6144,192]{0,1:T(8,128)(2,1)}, u32[]{:S(2)}) copy-start(bf16[6144,192]{0,1:T(8,128)(2,1)} %all-gather.7.cloned.1.call-done) | copy-start | bytes 7077892
  237.0 24.5 %copy-start.2 = (bf16[128,6144]{1,0:T(8,128)(2,1)S(1)}, bf16[128,6144]{1,0:T(8,128)(2,1)}, u32[]{:S(2)}) copy-start(bf16[128,6144]{1,0:T(8,128)(2,1)} %all-gather.5.cloned.1.call-done) | copy-start | bytes 4718596
  250.0 25.6 %all-to-all-start.1 = ((bf16[128,4,192]{0,2,1:T(8,128)(2,1)}), bf16[128,4,192]{0,2,1:T(8,128)(2,1)S(1)}, u32[]{:S(2)}, u32[]{:S(2)}) async-start(bf16[128,4,192]{0,2,1:T(8,128)(2,1)} %bitcast.13), calls=%async_computation.3 | async-start | bytes 393216 | tf_op jit(solution)/shard_map/all_to_all | solution.py:79
  262.9 17.8 %copy-start = (bf16[768,1536]{1,0:T(8,128)(2,1)S(1)}, bf16[768,1536]{1,0:T(8,128)(2,1)}, u32[]{:S(2)}) copy-start(bf16[768,1536]{1,0:T(8,128)(2,1)} %all-gather.9.cloned.1.call-done) | copy-start | bytes 7077892
  275.6 65.8 %all-to-all-start = ((bf16[128,4,1536]{2,0,1:T(8,128)(2,1)}), bf16[128,4,1536]{2,0,1:T(8,128)(2,1)}, u32[]{:S(2)}, u32[]{:S(2)}) async-start(bf16[128,4,1536]{2,0,1:T(8,128)(2,1)} %bitcast.44), calls=%async_computation.2 | async-start | bytes 3145728 | tf_op jit(solution)/shard_map/all_to_all | solution.py:78
  280.0 58.7 %all-gather.11.cloned.1.call-start = ((), (), s32[]{:S(2)}) async-start(), calls=%async_computation.9 | async-start | bytes 1966080 | tf_op jit(solution)/shard_map/all_gather | solution.py:81
  280.6 576.4 %all-reduce.5.cloned.1.call-start = ((), (), s32[]{:S(2)}) async-start(), calls=%async_computation.10 | async-start | bytes 3145728 | tf_op jit(solution)/shard_map/psum | solution.py:46
  326.3 530.7 %copy-start.3 = (bf16[128,1536]{1,0:T(8,128)(2,1)S(1)}, bf16[128,1536]{1,0:T(8,128)(2,1)}, u32[]{:S(2)}) copy-start(bf16[128,1536]{1,0:T(8,128)(2,1)} %param.6) | copy-start | bytes 1179652
  326.3 530.7 %copy-start.6 = (f32[1536]{0:T(1024)S(1)}, f32[1536]{0:T(1024)}, u32[]{:S(2)}) copy-start(f32[1536]{0:T(1024)} %param.8) | copy-start | bytes 18436
  341.4 524.5 %copy-start.5 = (bf16[128,1536]{1,0:T(8,128)(2,1)S(1)}, bf16[128,1536]{1,0:T(8,128)(2,1)}, u32[]{:S(2)}) copy-start(bf16[128,1536]{1,0:T(8,128)(2,1)} %param.7) | copy-start | bytes 1179652
Sparse Core Ops, SparseCore 0:
  10.1 85.8 all-gather.8
  98.7 25.3 all-gather.4
  126.2 82.6 all-gather.6
  212.1 19.5 reduce-scatter.2
  237.1 45.0 reduce-scatter.4
  284.4 54.2 all-gather.10
  341.9 515.0 all-reduce.4
where the time goes:
time: 878 us; the launch traced here: 875 us
  waiting for transfers between devices  744 us (85%)
  blocking collectives  76.2 us (9%)
  starting transfers between devices  16.1 us (2%)
  matrix products  16.1 us (2%)
  between operations  14.2 us (2%)
    psum x1, waiting for transfers between devices, per_device(): branch_total = lax.psum(branch_part, 'section')  513 us
    all_gather x1, waiting for transfers between devices, per_device(): lax.all_gather(w_in, 'row', axis=0, tiled=True)  84.8 us
    all_gather x1, waiting for transfers between devices, per_device(): lax.all_gather(w_out, 'row', axis=0, tiled=True)  71.6 us
    all_gather x1, blocking collectives, per_device(): hid_rows = lax.all_gather(grad_hid, 'row', axis=0, tiled=True)  43.3 us
    all_gather x1, waiting for transfers between devices, per_device(): lax.all_gather((scaled * ln_gain + ln_bias).astype(jnp.bfloat16), 'col',...  24.8 us
    reduce_scatter x1, waiting for transfers between devices, per_device(): lax.psum_scatter(lax.dot_general(panel_rows, cotangent, (((1,), (1,)), ((...  22.9 us
  transfers between devices with their start and end apart: 9, of which 7 were waited for; matrix products, arithmetic and copies ran while one was open for 2% of the time, Pallas kernels for 0%

commit v1 on v0

v1 whole, which is shorter than its diff:
```python
import functools

import jax
import jax.numpy as jnp
from jax import lax
from jax.experimental import pallas as pl
from jax.experimental.pallas import tpu as pltpu
from jax.sharding import PartitionSpec as P

EPS = 1e-05
SLOPE = 0.7978845608028654
CUBIC = 0.044715
F32, BF16 = jnp.float32, jnp.bfloat16
NX, NY, NZ, NL = 4, 4, 16, 8
TOK, FEAT, HIDT = 128, 1536, 192
D = NX * FEAT
QR = TOK // NY
PR, PC = TOK // NL, FEAT // NY
VMEM = pl.BlockSpec(memory_space=pltpu.VMEM)
NT = (((1,), (1,)), ((), ()))
TN = (((0,), (0,)), ((), ()))


def gelu_both(values):
    inner = jnp.tanh(SLOPE * (values + CUBIC * values * values * values))
    act = 0.5 * values * (1.0 + inner)
    slope = 0.5 * (1.0 + inner) + 0.5 * values * (1.0 - inner * inner) * SLOPE * (
        1.0 + 3.0 * CUBIC * values * values
    )
    return act, slope


def place():
    section, row, x = lax.axis_index("section"), lax.axis_index("row"), lax.axis_index("col")
    y, zl = lax.div(section, NL), lax.rem(section, NL)
    zh, k = lax.div(row, 2), lax.rem(row, 2)
    return x, y, zh * NL + zl, zh, zl, k, row


def dev(x, y, z, k):
    return (y * NL + lax.rem(z, NL), lax.div(z, NL) * 2 + k, x)


def send(src, dst, ssem, rsem, to):
    copy = pltpu.make_async_remote_copy(
        src_ref=src, dst_ref=dst, send_sem=ssem, recv_sem=rsem,
        device_id=to, device_id_type=pl.DeviceIdType.MESH,
    )
    copy.start()
    return copy


def arrived(ref, sem):
    pltpu.make_async_copy(ref, ref, sem).wait()


def meet(peers, turned=None, diag=None):
    barrier = pltpu.get_barrier_semaphore()

    def greet(some):
        for peer in some:
            pl.semaphore_signal(barrier, inc=1, device_id=peer, device_id_type=pl.DeviceIdType.MESH)
        pl.semaphore_wait(barrier, len(some))

    if turned is None:
        greet(peers)
    else:
        pl.when(diag)(lambda: greet(peers))
        pl.when(jnp.logical_not(diag))(lambda: greet(peers + [turned]))


def al(value, mult):
    return pl.multiple_of(value, mult)


def pack_pair(first, second):
    lane = lax.broadcasted_iota(jnp.int32, (TOK, TOK), 1)
    both = jnp.where(lane == 0, first, jnp.where(lane == 1, second, 0.0))
    return both.T[0:8, :]


def unpack_pair(packed):
    both = jnp.concatenate([packed, jnp.zeros((TOK - 8, TOK), F32)], axis=0).T
    return both[:, 0:1], both[:, 1:2]


def share_kernel(x_ref, cot_ref, gain_ref, bias_ref, X, C, st_ref, xn, sums, ssem, rsem):
    x, y, z, zh, zl, k, r = place()
    zm = NZ - 1 - z
    xs = [lax.rem(x + d, NX) for d in (1, 2, 3)]
    ys = [lax.rem(y + d, NY) for d in (1, 2, 3)]
    meet(
        [dev(p, y, z, k) for p in xs]
        + [dev(x, p, z, k) for p in ys]
        + [dev(x, y, z, 1 - k), dev(x, y, zm, k), dev(x, y, zm, 1 - k)]
    )
    q = pl.ds(al(y * QR, QR), QR)
    sent = []
    tile_of = [zh * 2 + k, zh * 2 + 1 - k, (1 - zh) * 2 + k, (1 - zh) * 2 + 1 - k]
    sent.append(send(cot_ref.at[q], C.at[r, q], ssem.at[0], rsem.at[0], dev(x, y, zm, k)))
    sent.append(send(cot_ref, C.at[r], ssem.at[1], rsem.at[1], dev(x, y, z, 1 - k)))
    rows = x_ref[...].astype(F32)
    sums[0] = pack_pair(
        jnp.sum(rows, -1, keepdims=True), jnp.sum(rows * rows, -1, keepdims=True)
    )
    for i, p in enumerate(xs):
        sent.append(send(sums.at[0], sums.at[1 + i], ssem.at[2 + i], rsem.at[2 + i], dev(p, y, z, k)))
    C[r] = cot_ref[...]
    for i in range(3):
        arrived(sums.at[1 + i], rsem.at[2 + i])
    first, second = unpack_pair((sums[0] + sums[1]) + (sums[2] + sums[3]))
    mean = first / D
    rstd = lax.rsqrt(second / D - mean * mean + EPS)
    lane = lax.broadcasted_iota(jnp.int32, (TOK, TOK), 1)
    st_ref[...] = jnp.where(lane == 0, mean, rstd)
    xn[...] = ((x_ref[...].astype(F32) - mean) * rstd * gain_ref[...] + bias_ref[...]).astype(BF16)
    diag = r == x
    zb, kb = lax.div(x, 2), lax.rem(x, 2)
    across = (zb != zh).astype(jnp.int32)
    delta = across * 2 + (kb != k).astype(jnp.int32)
    ztarget = zb * NL + jnp.where(zb == zh, zl, NL - 1 - zl)
    XQ, YQ, YC = 5, 9, 21

    @pl.when(jnp.logical_not(diag))
    def _():
        send(xn.at[q], X.at[r, q], ssem.at[5], rsem.at[XQ + delta], dev(x, y, ztarget, kb))

    @pl.when(diag)
    def _():
        X[r, q, :] = xn[q, :]

    def cot_out():
        arrived(C.at[tile_of[2], q], rsem.at[0])
        for i, p in enumerate(ys):
            part = C.at[tile_of[2], q]
            sent.append(send(part, part, ssem.at[30 + i], rsem.at[YC + i], dev(x, p, z, k)))

    for d in range(4):
        part = X.at[tile_of[d], q]
        if d == 0:
            @pl.when(jnp.logical_not(diag))
            def _():
                arrived(part, rsem.at[XQ])
        else:
            arrived(part, rsem.at[XQ + d])

        @pl.when(diag)
        def _():
            for i, p in enumerate(xs):
                send(part, part, ssem.at[6 + d * 3 + i], rsem.at[XQ + d], dev(p, y, z, k))

        for i, p in enumerate(ys):
            sent.append(
                send(part, part, ssem.at[18 + d * 3 + i], rsem.at[YQ + d * 3 + i], dev(x, p, z, k))
            )
        if d == 1:
            cot_out()
    for i in range(3):
        src_y = lax.rem(y + NY - 1 - i, NY)
        arrived(C.at[tile_of[2], pl.ds(al(src_y * QR, QR), QR)], rsem.at[YC + i])
    sent.append(send(C.at[tile_of[2]], C.at[tile_of[2]], ssem.at[33], rsem.at[24], dev(x, y, z, 1 - k)))
    for d in range(4):
        for i in range(3):
            src_y = lax.rem(y + NY - 1 - i, NY)
            arrived(X.at[tile_of[d], pl.ds(al(src_y * QR, QR), QR)], rsem.at[YQ + d * 3 + i])
    arrived(C.at[tile_of[1]], rsem.at[1])
    arrived(C.at[tile_of[3]], rsem.at[24])
    for copy in sent:
        copy.wait_send()

    @pl.when(diag)
    def _():
        for d in range(4):
            for i in range(3):
                arrived(X.at[tile_of[d], q], ssem.at[6 + d * 3 + i])

    @pl.when(jnp.logical_not(diag))
    def _():
        arrived(xn.at[q], ssem.at[5])


def hidden_kernel(X, C, w_in, w_out, aT, gT, hs, hr, us, ur, gs, gr, ts, tr, av, ssem, rsem):
    x, y, z, zh, zl, k, r = place()
    zp = (1 - zh) * NL + zl
    xs = [lax.rem(x + d, NX) for d in (1, 2, 3)]
    diag = r == x
    core, pair = dev(x, y, z, 1 - k), dev(x, y, zp, k)
    turned = (lax.axis_index("section"), x, r)
    meet([dev(p, y, z, k) for p in xs] + [core, pair], turned, diag)
    sent = []

    def hid(t):
        return lax.dot_general(w_in[...], X[t], NT, preferred_element_type=F32)

    def grad(t):
        return lax.dot_general(w_out[...], C[t], NT, preferred_element_type=F32)

    for i, t in enumerate(((1 - zh) * 2 + 1 - k, zh * 2 + 1 - k)):
        hs[i] = hid(t)
        sent.append(send(hs.at[i], hr.at[i], ssem.at[i], rsem.at[i], core))
    for i in (1, 0, 2):
        gs[i] = grad(xs[i]).astype(BF16)
        sent.append(send(gs.at[i], gr.at[i], ssem.at[2 + i], rsem.at[2 + i], dev(xs[i], y, z, k)))
    far = hid((1 - zh) * 2 + k)
    arrived(hr.at[0], rsem.at[0])
    us[...] = (far + hr[0]).astype(BF16)
    sent.append(send(us, ur, ssem.at[5], rsem.at[5], pair))
    own_grad = grad(x)
    for i in range(3):
        arrived(gr.at[i], rsem.at[2 + i])
    own_grad = own_grad + gr[0].astype(F32) + gr[1].astype(F32) + gr[2].astype(F32)
    ts[...] = own_grad.astype(BF16)

    @pl.when(diag)
    def _():
        tr[...] = ts[...]

    @pl.when(jnp.logical_not(diag))
    def _():
        send(ts, tr, ssem.at[6], rsem.at[6], turned)

    near = hid(r)
    arrived(hr.at[1], rsem.at[1])
    near = near + hr[1]
    arrived(ur, rsem.at[5])
    act, slope = gelu_both(near + ur[...].astype(F32))
    av[...] = act.astype(BF16)

    @pl.when(diag)
    def _():
        aT[r] = av[...]

    @pl.when(jnp.logical_not(diag))
    def _():
        send(av, aT.at[r], ssem.at[7], rsem.at[7], turned)
        arrived(tr, rsem.at[6])

    gT[r] = (tr[...].astype(F32) * slope).astype(BF16)
    sent.append(send(gT.at[r], gT.at[r], ssem.at[8], rsem.at[8], pair))
    sent.append(send(gT.at[r], gT.at[r], ssem.at[9], rsem.at[9], core))

    @pl.when(jnp.logical_not(diag))
    def _():
        arrived(aT.at[x], rsem.at[7])

    for i, p in enumerate(xs):
        sent.append(send(aT.at[x], aT.at[x], ssem.at[10 + i], rsem.at[10 + i], dev(p, y, z, k)))
    other = (1 - zh) * 2 + k
    arrived(gT.at[other], rsem.at[8])
    sent.append(send(gT.at[other], gT.at[other], ssem.at[13], rsem.at[13], core))
    arrived(gT.at[zh * 2 + 1 - k], rsem.at[9])
    for i in range(3):
        arrived(aT.at[lax.rem(x + NX - 1 - i, NX)], rsem.at[10 + i])
    arrived(gT.at[(1 - zh) * 2 + 1 - k], rsem.at[13])
    for copy in sent:
        copy.wait_send()

    @pl.when(jnp.logical_not(diag))
    def _():
        arrived(ts, ssem.at[6])
        arrived(av, ssem.at[7])


def total_kernel(
    aT, gT, w_in, w_out, X, C, x_ref, cot_ref, st_ref, gain_ref,
    out, gx, g_in, g_out,
    gs, gr, g0, g1, g1r, g2, g2r, gp, gn,
    os, orr, o0, o1, o1r, o2, o2r, sums,
    ssem, rsem,
):
    x, y, z, zh, zl, k, r = place()
    xs = [lax.rem(x + d, NX) for d in (1, 2, 3)]
    ys = [lax.rem(y + d, NY) for d in (1, 2, 3)]
    zs = [lax.rem(z + d, NZ) for d in range(1, NZ)]
    ls = [lax.rem(zl + d, NL) for d in range(1, NL)]
    diag = r == x
    core = dev(x, y, z, 1 - k)
    turned = (lax.axis_index("section"), x, r)
    meet(
        [dev(p, y, z, k) for p in xs] + [dev(x, p, z, k) for p in ys]
        + [dev(x, y, p, k) for p in zs] + [core],
        turned, diag,
    )
    sent = []
    count = [0]

    def put(src, dst, rslot, to):
        sent.append(send(src, dst, ssem.at[count[0]], rsem.at[rslot], to))
        count[0] += 1

    GX, OC, OY, GY, OZ, GL, GT = 0, 3, 5, 8, 11, 26, 33
    OAL, OAY, GAL, GAY, ST = 34, 41, 44, 51, 54

    def part_g(t):
        return lax.dot_general(gT[t], w_in[...], TN, preferred_element_type=F32)

    def part_o(t):
        return lax.dot_general(aT[t], w_out[...], TN, preferred_element_type=F32)

    def cols(p):
        return pl.ds(al(p * PC, PC), PC)

    def prow(p):
        return pl.ds(al(p * PR, PR), PR)

    for i in (1, 0, 2):
        gs[i] = part_g(xs[i]).astype(BF16)
        put(gs.at[i], gr.at[i], GX + i, dev(xs[i], y, z, k))
    for i in range(2):
        os[i] = part_o(i * 2 + 1 - k).astype(BF16)
        put(os.at[i], orr.at[i], OC + i, core)
    for i in range(2):
        o0[i] = part_o(i * 2 + k)
    for i in range(2):
        arrived(orr.at[i], rsem.at[OC + i])
    o1[...] = (o0[...] + orr[...].astype(F32)).astype(BF16)
    for i, p in enumerate(ys):
        put(o1.at[:, :, cols(p)], o1r.at[i], OY + i, dev(x, p, z, k))
    g0[...] = part_g(x)
    acc = jnp.zeros((HIDT, FEAT), F32)
    for t in range(4):
        acc = acc + jnp.dot(aT[t], C[t], preferred_element_type=F32)
    g_out[...] = acc.astype(BF16)
    for i in range(3):
        arrived(o1r.at[i], rsem.at[OY + i])
    o2[...] = (
        o1[:, :, cols(y)].astype(F32) + o1r[0].astype(F32) + o1r[1].astype(F32) + o1r[2].astype(F32)
    ).astype(BF16)
    for i, p in enumerate(zs):
        put(o2.at[lax.div(p, NL), prow(lax.rem(p, NL))], o2r.at[i], OZ + i, dev(x, y, p, k))
    acc = jnp.zeros((HIDT, FEAT), F32)
    for t in range(4):
        acc = acc + jnp.dot(gT[t], X[t], preferred_element_type=F32)
    g_in[...] = acc.astype(BF16)
    for i in range(3):
        arrived(gr.at[i], rsem.at[GX + i])
    g1[...] = (g0[...] + gr[0].astype(F32) + gr[1].astype(F32) + gr[2].astype(F32)).astype(BF16)
    for i, p in enumerate(ys):
        put(g1.at[:, cols(p)], g1r.at[i], GY + i, dev(x, p, z, k))
    for i in range(NZ - 1):
        arrived(o2r.at[i], rsem.at[OZ + i])
    piece = o2[zh, prow(zl), :].astype(F32)
    for i in range(NZ - 1):
        piece = piece + o2r[i].astype(F32)
    mine = (prow(zl), cols(y))
    out[mine] = (x_ref[mine].astype(F32) + piece).astype(BF16)
    for i, p in enumerate(ls):
        put(out.at[mine], out.at[mine], OAL + i, dev(x, y, zh * NL + p, k))
    for i in range(3):
        arrived(g1r.at[i], rsem.at[GY + i])
    g2[...] = (
        g1[:, cols(y)].astype(F32) + g1r[0].astype(F32) + g1r[1].astype(F32) + g1r[2].astype(F32)
    ).astype(BF16)
    for i, p in enumerate(ls):
        put(g2.at[prow(p)], g2r.at[i], GL + i, dev(x, y, zh * NL + p, k))
    for i in range(NL - 1):
        arrived(g2r.at[i], rsem.at[GL + i])
    piece = g2[prow(zl), :].astype(F32)
    for i in range(NL - 1):
        piece = piece + g2r[i].astype(F32)
    gp[...] = piece.astype(BF16)

    @pl.when(diag)
    def _():
        gn[mine] = gp[...]

    @pl.when(jnp.logical_not(diag))
    def _():
        send(gp, gn.at[mine], ssem.at[63], rsem.at[GT], turned)

    for i in range(NL - 1):
        src = lax.rem(zl + NL - 1 - i, NL)
        arrived(out.at[prow(src), cols(y)], rsem.at[OAL + i])
    for i, p in enumerate(ys):
        put(out.at[:, cols(y)], out.at[:, cols(y)], OAY + i, dev(x, p, z, k))

    @pl.when(jnp.logical_not(diag))
    def _():
        arrived(gn.at[mine], rsem.at[GT])

    for i, p in enumerate(ls):
        put(gn.at[mine], gn.at[mine], GAL + i, dev(x, y, zh * NL + p, k))
    for i in range(NL - 1):
        src = lax.rem(zl + NL - 1 - i, NL)
        arrived(gn.at[prow(src), cols(y)], rsem.at[GAL + i])
    for i, p in enumerate(ys):
        put(gn.at[:, cols(y)], gn.at[:, cols(y)], GAY + i, dev(x, p, z, k))
    mean, rstd = st_ref[:, 0:1], st_ref[:, 1:2]
    scaled = (x_ref[...].astype(F32) - mean) * rstd
    for i in range(3):
        src = lax.rem(y + NY - 1 - i, NY)
        arrived(gn.at[:, cols(src)], rsem.at[GAY + i])
    gz = gn[...].astype(F32) * gain_ref[...]
    sums[0] = pack_pair(
        jnp.sum(gz, -1, keepdims=True), jnp.sum(gz * scaled, -1, keepdims=True)
    )
    for i, p in enumerate(xs):
        put(sums.at[0], sums.at[1 + i], ST + i, dev(p, y, z, k))
    for i in range(3):
        src = lax.rem(y + NY - 1 - i, NY)
        arrived(out.at[:, cols(src)], rsem.at[OAY + i])
    for i in range(3):
        arrived(sums.at[1 + i], rsem.at[ST + i])
    first, second = unpack_pair((sums[0] + sums[1]) + (sums[2] + sums[3]))
    delta = rstd * (gz - first / D - scaled * (second / D))
    gx[...] = (cot_ref[...].astype(F32) + delta).astype(BF16)
    for copy in sent:
        copy.wait_send()

    @pl.when(jnp.logical_not(diag))
    def _():
        arrived(gp, ssem.at[63])


def per_device(inputs, cotangent, ln_gain, ln_bias, w_in, w_out):
    gain, bias = ln_gain.reshape(1, FEAT), ln_bias.reshape(1, FEAT)
    w_in_t = w_in.T
    dma = pltpu.SemaphoreType.DMA

    def params(number):
        return pltpu.CompilerParams(
            collective_id=number, has_side_effects=True, vmem_limit_bytes=48 << 20
        )

    wide = jax.ShapeDtypeStruct((4, TOK, FEAT), BF16)
    X, C, stats = pl.pallas_call(
        share_kernel,
        name="share",
        out_shape=[wide, wide, jax.ShapeDtypeStruct((TOK, TOK), F32)],
        in_specs=[VMEM] * 4,
        out_specs=[VMEM] * 3,
        scratch_shapes=[
            pltpu.VMEM((TOK, FEAT), BF16),
            pltpu.VMEM((4, 8, TOK), F32),
            dma((34,)),
            dma((25,)),
        ],
        compiler_params=params(0),
    )(inputs, cotangent, gain, bias)
    small = jax.ShapeDtypeStruct((4, HIDT, TOK), BF16)
    one = pltpu.VMEM((HIDT, TOK), BF16)
    aT, gT = pl.pallas_call(
        hidden_kernel,
        name="hidden",
        out_shape=[small, small],
        in_specs=[VMEM] * 4,
        out_specs=[VMEM] * 2,
        scratch_shapes=[
            pltpu.VMEM((2, HIDT, TOK), F32),
            pltpu.VMEM((2, HIDT, TOK), F32),
            one, one,
            pltpu.VMEM((3, HIDT, TOK), BF16),
            pltpu.VMEM((3, HIDT, TOK), BF16),
            one, one, one,
            dma((14,)),
            dma((14,)),
        ],
        compiler_params=params(1),
    )(X, C, w_in_t, w_out)
    tile = jax.ShapeDtypeStruct((TOK, FEAT), BF16)
    grad = jax.ShapeDtypeStruct((HIDT, FEAT), BF16)

    def vb(*shape):
        return pltpu.VMEM(shape, BF16)

    out, gx, g_in, g_out = pl.pallas_call(
        total_kernel,
        name="total",
        out_shape=[tile, tile, grad, grad],
        in_specs=[VMEM] * 10,
        out_specs=[VMEM] * 4,
        scratch_shapes=[
            vb(3, TOK, FEAT), vb(3, TOK, FEAT), pltpu.VMEM((TOK, FEAT), F32),
            vb(TOK, FEAT), vb(3, TOK, PC), vb(TOK, PC), vb(NL - 1, PR, PC), vb(PR, PC), vb(TOK, FEAT),
            vb(2, TOK, FEAT), vb(2, TOK, FEAT), pltpu.VMEM((2, TOK, FEAT), F32),
            vb(2, TOK, FEAT), vb(3, 2, TOK, PC), vb(2, TOK, PC), vb(NZ - 1, PR, PC),
            pltpu.VMEM((4, 8, TOK), F32),
            dma((64,)),
            dma((57,)),
        ],
        compiler_params=params(2),
    )(aT, gT, w_in_t, w_out, X, C, inputs, cotangent, stats, gain)
    return out, gx, g_in.T, g_out


def solution(mesh):
    return jax.shard_map(
        per_device,
        mesh=mesh,
        in_specs=(
            P("row", "col"),
            P("row", "col"),
            P("col"),
            P("col"),
            P("row", ("section", "col")),
            P(("section", "row"), "col"),
        ),
        out_specs=(
            P("row", "col"),
            P("row", "col"),
            P("row", ("section", "col")),
            P(("section", "row"), "col"),
        ),
        check_vma=False,
    )
```

time: 878 us -> 161 us (0.18)
  waiting for transfers between devices: 744 us -> 0 us
  Pallas kernels: 0 us -> 150 us
  blocking collectives: 76.2 us -> 0 us
  matrix products: 16.1 us -> 0 us
  starting transfers between devices: 16.1 us -> 0 us
  between operations: 14.2 us -> 0.7 us
    psum x1 -> x0, waiting for transfers between devices: 513 us -> none  [per_device(): branch_total = lax.psum(branch_part, 'section')]
    all_gather x4 -> x0, waiting for transfers between devices: 194 us -> none  [the longest x1 84.8 us: per_device(): lax.all_gather(w_in, 'row', axis=0, tiled=True)]
    pallas_call x0 -> x3, Pallas kernels: none -> 150 us  [the longest x1 73.7 us: per_device(): pl.pallas_call(total_kernel, name='total', out_shape=[tile, tile, grad, g...]
    all_gather x2 -> x0, blocking collectives: 56.3 us -> none  [the longest x1 43.3 us: per_device(): hid_rows = lax.all_gather(grad_hid, 'row', axis=0, tiled=True)]
    reduce_scatter x2 -> x0, waiting for transfers between devices: 22.9 us -> none  [the longest x1 22.9 us: per_device(): lax.psum_scatter(lax.dot_general(panel_rows, cotangent, (((1,), (1,)), ((...]
    psum x2 -> x0, blocking collectives: 19.8 us -> none  [the longest x1 12.4 us: per_device(): lax.psum((jnp.sum(stream_f32, -1, keepdims=True), jnp.sum(stream_f32 * st...]
    dot_general x6 -> x0, matrix products: 16.1 us -> none  [the longest x1 3.18 us: per_device(): lax.dot_general(panel_rows, cotangent, (((1,), (1,)), ((), ())), preferre...]
    all_to_all x2 -> x0, starting transfers between devices: 15.8 us -> none  [the longest x1 11.5 us: per_device(): lax.all_to_all(active_row, 'row', split_axis=1, concat_axis=0, tiled=True)]
  transfers between devices with their start and end apart: 9 -> 0, of which waited for: 7 -> 0; matrix products, arithmetic and copies ran while one was open for 2% -> 0% of each run, Pallas kernels for 0% -> 0%
where the time goes in v1:
time: 161 us; the launch traced here: 160 us
  Pallas kernels  150 us (93%)
  local copies, waits for them, and re-layouts  9.08 us (6%)
    pallas_call x1, Pallas kernels, per_device(): pl.pallas_call(total_kernel, name='total', out_shape=[tile, tile, grad, g...  73.7 us
    pallas_call x1, Pallas kernels, per_device(): pl.pallas_call(share_kernel, name='share', out_shape=[wide, wide, jax.Sha...  45.1 us
    pallas_call x1, Pallas kernels, per_device(): pl.pallas_call(hidden_kernel, name='hidden', out_shape=[small, small], in...  31.1 us
    unnamed x18, local copies, waits for them, and re-layouts  7.67 us

profile of v1, /device:TPU:6, one launch (start us, length us, event | category | flops | bytes accessed | tf_op | source)
XLA Modules:
  0.0 159.7 jit_solution(13916705117857750742)
XLA Ops:
  0.6 0.7 reshape.14.gain_ref
  1.3 0.7 reshape.15.bias_ref
  2.0 0.0 copy-start.5
  2.0 1.0 copy-done.5
  3.0 0.0 copy-start.6
  3.0 1.0 copy-done.6
  4.0 45.1 %share.1 = (bf16[4,128,1536]{2,1,0:T(8,128)(2,1)S(1)}, bf16[4,128,1536]{2,1,0:T(8,128)(2,1)S(1)}, f32[128,128]{1,0:T(8,128)S(1)}) custom-call(bf16[128,1536]{1,0:T(8,128)(2,1)S(1)} %copy-done.5, bf16[128,1536]{1,0:T(8,128)(2,1)S(1)} %copy-done.6, f32[1,1536]{1,0:T(1,128)S(1)} %reshape.14.gain_ref, f32[1,1536]{1,0:T(1,128)S(1)} %reshape.15.bias_ref), custom_call_target="tpu_custom_call" | custom-call | tf_op jit(solution)/shard_map/share/pallas_call | solution.py:426
  49.2 0.0 copy-start
  49.2 0.0 copy-start.1
  49.2 1.5 copy-done.1
  50.7 0.0 copy-start.3
  50.7 1.1 copy-done.3
  51.7 0.0 copy-start.2
  51.7 0.0 copy-start.4
  51.8 31.1 %hidden.1 = (bf16[4,192,128]{2,1,0:T(8,128)(2,1)S(1)}, bf16[4,192,128]{2,1,0:T(8,128)(2,1)S(1)}) custom-call(bf16[4,128,1536]{2,1,0:T(8,128)(2,1)S(1)} %get-tuple-element.13.X, bf16[4,128,1536]{2,1,0:T(8,128)(2,1)S(1)} %get-tuple-element.14.C, bf16[192,1536]{1,0:T(8,128)(2,1)S(1)} %bitcast.2, bf16[192,1536]{1,0:T(8,128)(2,1)S(1)} %copy-done.3), custom_call_target="tpu_custom_call" | custom-call | tf_op jit(solution)/shard_map/hidden/pallas_call | solution.py:442
  82.8 0.0 copy-done
  82.9 0.0 copy-done.2
  82.9 0.0 copy-done.4
  82.9 73.7 %total.1 = (bf16[128,1536]{1,0:T(8,128)(2,1)S(1)}, bf16[128,1536]{1,0:T(8,128)(2,1)S(1)}, bf16[192,1536]{1,0:T(8,128)(2,1)S(1)}, bf16[192,1536]{1,0:T(8,128)(2,1)S(1)}) custom-call(bf16[4,192,128]{2,1,0:T(8,128)(2,1)S(1)} %get-tuple-element.15.aT, bf16[4,192,128]{2,1,0:T(8,128)(2,1)S(1)} %get-tuple-element.16.gT, bf16[192,1536]{1,0:T(8,128)(2,1)S(1)} %bitcast.3, ...), custom_call_target="tpu_custom_call" | custom-call | tf_op jit(solution)/shard_map/total/pallas_call | solution.py:466
  156.6 0.7 copy.14
  157.4 0.7 copy.15
  158.1 0.8 copy.16
  158.9 0.8 copy.17
Async XLA Ops:
  2.0 1.0 copy-start.5
  3.0 1.0 copy-start.6
  49.2 33.7 %copy-start = (bf16[4,128,1536]{2,1,0:T(8,128)(2,1)}, bf16[4,128,1536]{2,1,0:T(8,128)(2,1)S(1)}, u32[]{:S(2)}) copy-start(bf16[4,128,1536]{2,1,0:T(8,128)(2,1)S(1)} %get-tuple-element.14.C) | copy-start | bytes 4718596
  49.2 1.5 copy-start.1
  50.7 1.1 copy-start.3
  51.7 31.1 %copy-start.2 = (bf16[1536,192]{0,1:T(8,128)(2,1)S(1)}, bf16[1536,192]{0,1:T(8,128)(2,1)}, u32[]{:S(2)}) copy-start(bf16[1536,192]{0,1:T(8,128)(2,1)} %param.10) | copy-start | bytes 1769476
  51.7 31.1 %copy-start.4 = (bf16[192,1536]{1,0:T(8,128)(2,1)S(1)}, bf16[192,1536]{1,0:T(8,128)(2,1)}, u32[]{:S(2)}) copy-start(bf16[192,1536]{1,0:T(8,128)(2,1)} %w_out.3) | copy-start | bytes 1769476

commit v2 on v0

v2 whole, which is shorter than its diff:
```python
import jax
import jax.numpy as jnp
from jax import lax
from jax.experimental import pallas as pl
from jax.experimental.pallas import tpu as pltpu
from jax.sharding import PartitionSpec as P

EPS = 1e-05
SLOPE = 0.7978845608028654
CUBIC = 0.044715
F32, BF16 = jnp.float32, jnp.bfloat16
NX, NY, NZ, NL = 4, 4, 16, 8
TOK, FEAT, HIDT = 128, 1536, 192
D = NX * FEAT
QR = TOK // NY
PR, PC = TOK // NL, FEAT // NY
ANY = pl.BlockSpec(memory_space=pl.ANY)
NT = (((1,), (1,)), ((), ()))


def gelu_both(values):
    inner = jnp.tanh(SLOPE * (values + CUBIC * values * values * values))
    act = 0.5 * values * (1.0 + inner)
    slope = 0.5 * (1.0 + inner) + 0.5 * values * (1.0 - inner * inner) * SLOPE * (
        1.0 + 3.0 * CUBIC * values * values
    )
    return act, slope


def place():
    section, row, x = lax.axis_index("section"), lax.axis_index("row"), lax.axis_index("col")
    y, zl = lax.div(section, NL), lax.rem(section, NL)
    zh, k = lax.div(row, 2), lax.rem(row, 2)
    return x, y, zh * NL + zl, zh, zl, k, row


def dev(x, y, z, k):
    return (y * NL + lax.rem(z, NL), lax.div(z, NL) * 2 + k, x)

def al(value, mult):
    return pl.multiple_of(value, mult)


def pack_pair(first, second):
    lane = lax.broadcasted_iota(jnp.int32, (TOK, TOK), 1)
    both = jnp.where(lane == 0, first, jnp.where(lane == 1, second, 0.0))
    return both.T[0:8, :]


def unpack_pair(packed):
    both = jnp.concatenate([packed, jnp.zeros((TOK - 8, TOK), F32)], axis=0).T
    return both[:, 0:1], both[:, 1:2]


def arrived(ref, sem):
    pltpu.make_async_copy(ref, ref, sem).wait()


class Wires:
    def __init__(self, ssem, rsem):
        self.ssem, self.rsem = ssem, rsem
        self.slots, self.sent = {}, []

    def slot(self, *name):
        return self.rsem.at[self.slots.setdefault(name, len(self.slots))]

    def put(self, make, name, pred=None):
        rsem, ssem = self.slot(*name), self.ssem.at[len(self.sent)]

        src, dst, to = make()

        def copy():
            return pltpu.make_async_remote_copy(
                src_ref=src, dst_ref=dst, send_sem=ssem, recv_sem=rsem,
                device_id=to, device_id_type=pl.DeviceIdType.MESH,
            )

        when(pred, lambda: copy().start())
        self.sent.append((pred, copy))

    def got(self, make, name, pred=None):
        ref, sem = make(), self.slot(*name)
        when(pred, lambda: arrived(ref, sem))

    def finish(self):
        for pred, copy in self.sent:
            when(pred, lambda copy=copy: copy().wait_send())


def when(pred, act):
    if pred is None:
        act()
    else:
        pl.when(pred)(act)


def tpos(t):
    return lax.rem(t, 2) * 2 + lax.div(t, 2)


N_SEND, N_RECV = 190, 160


def layer_kernel(
    x_any, cot_any, gain_any, bias_any, win_any, wout_any,
    out_any, gx_any, gin_any, gout_any,
    x_ref, cot_ref, gain_ref, bias_ref, w_in, w_out,
    X, C, xn, sums, st_ref,
    hs, hr, us, ur, qs, qr, ts, tr, gT, aT, gt, at,
    gs, gr, g0, g1, g1r, g2, g2r, gp, gn,
    os, orr, o0, o1, o1r, o2, o2r, stats, out, gx, g_in, g_out,
    ssem, rsem, lsem,
):
    x, y, z, zh, zl, k, r = place()
    no = jnp.logical_not
    w = Wires(ssem, rsem)
    put, got = w.put, w.got
    loads = [
        pltpu.make_async_copy(src, dst, lsem.at[i])
        for i, (src, dst) in enumerate((
            (x_any, x_ref), (cot_any, cot_ref), (gain_any, gain_ref),
            (bias_any, bias_ref), (win_any, w_in), (wout_any, w_out),
        ))
    ]
    for load in loads:
        load.start()
    zm, zp = NZ - 1 - z, (1 - zh) * NL + zl
    par = lax.rem(zl, 2)
    zn = z + 1 - 2 * par
    xs = [lax.rem(x + d, NX) for d in (1, 2, 3)]
    ys = [lax.rem(y + d, NY) for d in (1, 2, 3)]
    zs = [lax.rem(z + d, NZ) for d in range(1, NZ)]
    ls = [lax.rem(zl + d, NL) for d in range(NL)]
    diag = r == x
    zb, kb = lax.div(x, 2), lax.rem(x, 2)
    home = zb == zh
    beside = jnp.logical_and(home, k != kb)
    core, pair = dev(x, y, z, 1 - k), dev(x, y, zp, k)

    barrier = pltpu.get_barrier_semaphore()

    def greet(peer, pred=None):
        when(pred, lambda: pl.semaphore_signal(
            barrier, inc=1, device_id=peer, device_id_type=pl.DeviceIdType.MESH))

    for p in zs:
        greet(dev(x, y, p, k))
    greet(core)
    greet(dev(x, y, zm, 1 - k))
    for dx in range(4):
        for dy in range(4):
            if dx or dy:
                greet(dev(lax.rem(x + dx, NX), lax.rem(y + dy, NY), z, k))
    section = lax.axis_index("section")
    for half in range(2):
        greet((section, x, half * 2 + k), no(jnp.logical_and(diag, zh == half)))
    greet(dev(r, y, z, 1 - k), no(diag))
    for d in range(NL):
        greet(dev(r, y, zh * NL + ls[d], kb), no(diag) if d == 0 else None)
    def num(flag):
        return flag.astype(jnp.int32)
    total = 15 + 2 + 15 + 2 - num(diag) + 3 * num(beside) + 16 * num(home) - num(diag)

    loads[0].wait()
    rows = x_ref[...].astype(F32)
    sums[0] = pack_pair(
        jnp.sum(rows, -1, keepdims=True), jnp.sum(rows * rows, -1, keepdims=True)
    )
    loads[1].wait()
    loads[2].wait()
    loads[3].wait()
    pl.semaphore_wait(barrier, total)

    def rows_at(start, size):
        return pl.ds(al(start, 16), size)

    mine8 = rows_at(y * QR + par * 16, 16)
    theirs8 = rows_at(y * QR + (1 - par) * 16, 16)
    quarter = rows_at(y * QR, QR)
    front, back = pl.ds(0, 64), rows_at(64 + y * 16, 16)
    tiles = [zh * 2 + k, zh * 2 + 1 - k, (1 - zh) * 2 + k, (1 - zh) * 2 + 1 - k]

    for i, p in enumerate(xs):
        put(lambda: (sums.at[0], sums.at[1 + i], dev(p, y, z, k)), ("stat", i))
    put(lambda: (cot_ref.at[mine8], C.at[r, mine8], dev(x, y, zm, k)), ("cz",))
    put(lambda: (cot_ref, C.at[r], core), ("cc",))
    C[r] = cot_ref[...]
    for i in range(3):
        got(lambda: sums.at[1 + i], ("stat", i))
    first, second = unpack_pair((sums[0] + sums[1]) + (sums[2] + sums[3]))
    mean = first / D
    rstd = lax.rsqrt(second / D - mean * mean + EPS)
    lane = lax.broadcasted_iota(jnp.int32, (TOK, TOK), 1)
    st_ref[...] = jnp.where(lane == 0, mean, rstd)
    gain = gain_ref[...].reshape(1, FEAT)
    bias = bias_ref[...].reshape(1, FEAT)
    xn[...] = ((x_ref[...].astype(F32) - mean) * rstd * gain + bias).astype(BF16)

    away = no(home)
    for j in range(2):
        put(lambda: (xn.at[mine8], X.at[r, mine8], dev(x, y, zm, k if j == 0 else 1 - k)),
            ("xz", j), jnp.logical_and(away, (k == kb) if j == 0 else (k != kb)))
    put(lambda: (xn.at[back], X.at[r, back], core), ("xb", 1), beside)
    put(lambda: (xn.at[front], X.at[r, front], core), ("xf", 1), beside)

    @pl.when(diag)
    def _():
        X[r, back, :] = xn[back, :]
        X[r, front, :] = xn[front, :]

    def spread(ref, name):
        for i, p in enumerate(xs):
            put(lambda: (ref, ref, dev(p, y, z, k)), name, diag)

    def along_y(ref, name):
        for i, p in enumerate(ys):
            put(lambda: (ref, ref, dev(x, p, z, k)), name + (i,))

    for d in range(2):
        ref = X.at[tiles[d], back]
        got(lambda: ref, ("xb", d), no(diag) if d == 0 else None)
        spread(ref, ("xb", d))
        along_y(ref, ("yb", d))
    spread(X.at[tiles[0], front], ("xf", 0))
    got(lambda: X.at[tiles[1], front], ("xf", 1), diag)
    spread(X.at[tiles[1], front], ("xf", 1))
    got(lambda: C.at[tiles[2], theirs8], ("cz",))
    put(lambda: (C.at[tiles[2], theirs8], C.at[tiles[2], theirs8], dev(x, y, zn, k)), ("cn",))
    for d in (2, 3):
        ref = X.at[tiles[d], theirs8]
        got(lambda: ref, ("xz", d - 2), diag)
        put(lambda: (ref, ref, dev(x, y, zn, k)), ("xn", d), diag)
    got(lambda: C.at[tiles[2], mine8], ("cn",))
    along_y(C.at[tiles[2], quarter], ("cy",))
    for d in (2, 3):
        got(lambda: X.at[tiles[d], mine8], ("xn", d), diag)
        spread(X.at[tiles[d], quarter], ("xq", d))
    for d in (2, 3):
        ref = X.at[tiles[d], quarter]
        got(lambda: ref, ("xq", d), no(diag))
        along_y(ref, ("yq", d))
    from_y = [lax.rem(y + NY - 1 - i, NY) for i in range(3)]
    from_x = [lax.rem(x + NX - 1 - i, NX) for i in range(3)]

    loads[4].wait()
    loads[5].wait()
    for d in range(2):
        got(lambda: X.at[tiles[d], front], ("xf", d), no(diag))
        for i in range(3):
            got(lambda: X.at[tiles[d], rows_at(64 + from_y[i] * 16, 16)], ("yb", d, i))

    def hid(t):
        return lax.dot_general(w_in[...], X[t], NT, preferred_element_type=F32)

    def grad(t):
        return lax.dot_general(w_out[...], C[t], NT, preferred_element_type=F32)

    hs[0] = hid(tiles[1])
    put(lambda: (hs.at[0], hr.at[0], core), ("hc", 0))
    near = hid(tiles[0])
    for i in range(3):
        got(lambda: C.at[tiles[2], rows_at(from_y[i] * QR, QR)], ("cy", i))
    put(lambda: (C.at[tiles[2]], C.at[tiles[2]], core), ("cf",))
    got(lambda: hr.at[0], ("hc", 0))
    h_near = near + hr[0]
    us[0] = h_near.astype(BF16)
    put(lambda: (us.at[0], ur.at[1], pair), ("hz", 0))
    hs[2] = h_near
    got(lambda: C.at[tiles[1]], ("cc",))
    got(lambda: C.at[tiles[3]], ("cf",))
    for i in (1, 0, 2):
        qs[i] = grad(xs[i]).astype(BF16)
        put(lambda: (qs.at[i], qr.at[i], dev(xs[i], y, z, k)), ("ga", i))
    own = grad(x)
    for i in range(3):
        got(lambda: qr.at[i], ("ga", i))
    ts[...] = (own + qr[0].astype(F32) + qr[1].astype(F32) + qr[2].astype(F32)).astype(BF16)
    for half in range(2):
        selfish = jnp.logical_and(diag, zh == half)
        for side in range(2):
            put(lambda: (ts, tr.at[side], (section, half * 2 + kb, r)), ("gt", side),
                jnp.logical_and(no(selfish), zb == side))

    @pl.when(diag)
    def _():
        tr[zh] = ts[...]

    for d in (2, 3):
        for i in range(3):
            got(lambda: X.at[tiles[d], rows_at(from_y[i] * QR, QR)], ("yq", d, i))
    hs[1] = hid(tiles[3])
    put(lambda: (hs.at[1], hr.at[1], core), ("hc", 1))
    far = hid(tiles[2])
    got(lambda: hr.at[1], ("hc", 1))
    h_far = far + hr[1]
    us[1] = h_far.astype(BF16)
    put(lambda: (us.at[1], ur.at[0], pair), ("hz", 1))
    hs[3] = h_far
    for side in range(2):
        got(lambda: tr.at[side], ("gt", side), no(jnp.logical_and(diag, zh == side)))

    def activate(step, half):
        act, slope = gelu_both(hs[2 + step] + ur[step].astype(F32))
        gT[k * 2 + half] = (tr[half].astype(F32) * slope).astype(BF16)
        at[half] = act.astype(BF16)

    got(lambda: ur.at[1], ("hz", 0))
    activate(1, 1 - zh)
    put(lambda: (gT.at[k * 2 + 1 - zh], gT.at[k * 2 + 1 - zh], core), ("gc", 1))
    got(lambda: ur.at[0], ("hz", 1))
    activate(0, zh)
    put(lambda: (gT.at[k * 2 + zh], gT.at[k * 2 + zh], core), ("gc", 0))
    held = pl.ds(k * 2, 2)
    for i, p in enumerate(xs):
        put(lambda: (at, aT.at[held], dev(p, y, z, k)), ("ax", 0), diag)
    for i, p in enumerate(xs):
        put(lambda: (at, aT.at[held], dev(p, y, z, 1 - k)), ("ax", 1), beside)
    put(lambda: (at, aT.at[held], core), ("ax", 1), beside)

    @pl.when(diag)
    def _():
        aT[held] = at[...]

    def cols(p):
        return pl.ds(al(p * PC, PC), PC)

    def prow(p):
        return pl.ds(al(p * PR, PR), PR)

    got(lambda: gT.at[(1 - k) * 2 + 1 - zh], ("gc", 1))
    got(lambda: gT.at[(1 - k) * 2 + zh], ("gc", 0))

    for p in range(4):
        gt[p] = gT[p].T
    order = (2, 1, 3, 0)
    for j in order:
        c = cols(lax.rem(y + j, NY))
        for i in (1, 0, 2):
            gs[i, :, c] = jnp.dot(
                gt[tpos(xs[i])], w_in[:, c], preferred_element_type=F32).astype(BF16)
            put(lambda: (gs.at[i, :, c], gr.at[i, :, c], dev(xs[i], y, z, k)), ("gx", j, i))
    g0[...] = jnp.dot(gt[tpos(x)], w_in[...], preferred_element_type=F32)

    got(lambda: aT.at[held], ("ax", 0), no(diag))
    got(lambda: aT.at[pl.ds((1 - k) * 2, 2)], ("ax", 1))
    for p in range(4):
        gt[p] = aT[p].T
    for i in range(2):
        os[i] = jnp.dot(
            gt[(1 - k) * 2 + i], w_out[...], preferred_element_type=F32).astype(BF16)
        put(lambda: (os.at[i], orr.at[i], core), ("oc", i))
    for i in range(2):
        o0[i] = jnp.dot(gt[k * 2 + i], w_out[...], preferred_element_type=F32)
    for i in range(2):
        got(lambda: orr.at[i], ("oc", i))
    o1[...] = (o0[...] + orr[...].astype(F32)).astype(BF16)
    for i, p in enumerate(ys):
        put(lambda: (o1.at[:, :, cols(p)], o1r.at[i], dev(x, p, z, k)), ("oy", i))

    acc = jnp.zeros((HIDT, FEAT), F32)
    for t in range(4):
        acc = acc + jnp.dot(aT[(t % 2) * 2 + t // 2], C[t], preferred_element_type=F32)
    g_out[...] = acc.astype(BF16)
    stores = [pltpu.make_async_copy(g_out, gout_any, lsem.at[6])]
    stores[0].start()

    def sum_x(j):
        c = cols(lax.rem(y + j, NY))
        for i in range(3):
            got(lambda: gr.at[i, :, c], ("gx", j, i))
        g1[:, c] = (
            g0[:, c] + gr[0, :, c].astype(F32) + gr[1, :, c].astype(F32) + gr[2, :, c].astype(F32)
        ).astype(BF16)
        if j:
            put(lambda: (g1.at[:, c], g1r.at[j - 1], dev(x, lax.rem(y + j, NY), z, k)), ("gy", j))

    sum_x(2)
    acc = jnp.zeros((HIDT, FEAT), F32)
    for t in range(4):
        acc = acc + jnp.dot(gT[(t % 2) * 2 + t // 2], X[t], preferred_element_type=F32)
    g_in[...] = acc.astype(BF16)
    stores.append(pltpu.make_async_copy(g_in, gin_any, lsem.at[7]))
    stores[1].start()
    sum_x(1)
    for i in range(3):
        got(lambda: o1r.at[i], ("oy", i))
    o2[...] = (
        o1[:, :, cols(y)].astype(F32) + o1r[0].astype(F32) + o1r[1].astype(F32) + o1r[2].astype(F32)
    ).astype(BF16)
    for i, p in enumerate(zs):
        put(lambda: (o2.at[lax.div(p, NL), prow(lax.rem(p, NL))], o2r.at[i], dev(x, y, p, k)),
            ("oz", i))
    sum_x(3)
    sum_x(0)
    for j in (1, 2, 3):
        got(lambda: g1r.at[j - 1], ("gy", j))
    g2[...] = (
        g1[:, cols(y)].astype(F32) + g1r[0].astype(F32) + g1r[1].astype(F32) + g1r[2].astype(F32)
    ).astype(BF16)
    for d in range(NL):
        put(lambda: (g2.at[prow(ls[d])], g2r.at[1, d], dev(x, y, zp - zl + ls[d], k)),
            ("gzo", d), away)
        if d:
            put(lambda: (g2.at[prow(ls[d])], g2r.at[0, d], dev(x, y, zh * NL + ls[d], k)),
                ("gzs", d), home)
    mine = (prow(zl), cols(y))
    for i in range(NZ - 1):
        got(lambda: o2r.at[i], ("oz", i))
    piece = o2[zh, prow(zl), :].astype(F32)
    for i in range(NZ - 1):
        piece = piece + o2r[i].astype(F32)
    out[mine] = (x_ref[mine].astype(F32) + piece).astype(BF16)
    for d in range(1, NL):
        put(lambda: (out.at[mine], out.at[mine], dev(x, y, zh * NL + ls[d], k)), ("oal", d))

    @pl.when(home)
    def _():
        for d in range(NL):
            arrived(g2r.at[1, d], w.slot("gzo", d))
            if d:
                arrived(g2r.at[0, d], w.slot("gzs", d))
        same, other = g2[prow(zl), :].astype(F32), g2r[1, 0].astype(F32)
        for d in range(1, NL):
            same = same + g2r[0, d].astype(F32)
            other = other + g2r[1, d].astype(F32)
        gp[0] = same.astype(BF16)
        gp[1] = other.astype(BF16)

    for d in range(NL):
        for j in range(2):
            target = dev((zh if j == 0 else 1 - zh) * 2 + k, y, zh * NL + ls[d], kb)
            put(lambda: (gp.at[j], gn.at[mine], target), ("gal", d),
                beside_or_far(home, diag, d, j))

    @pl.when(diag)
    def _():
        gn[mine] = gp[0]

    from_l = [lax.rem(zl + NL - d, NL) for d in range(NL)]
    for d in range(1, NL):
        got(lambda: out.at[prow(from_l[d]), cols(y)], ("oal", d))
    for i, p in enumerate(ys):
        put(lambda: (out.at[:, cols(y)], out.at[:, cols(y)], dev(x, p, z, k)), ("oay", i))
    mean, rstd = st_ref[:, 0:1], st_ref[:, 1:2]
    scaled = (x_ref[...].astype(F32) - mean) * rstd
    g0[...] = scaled
    for d in range(NL):
        got(lambda: gn.at[prow(from_l[d]), cols(y)], ("gal", d), no(diag) if d == 0 else None)
    for i, p in enumerate(ys):
        put(lambda: (gn.at[:, cols(y)], gn.at[:, cols(y)], dev(x, p, z, k)), ("gay", i))
    gain_row = gain_cols(gain, y)
    gz = gn[:, cols(y)].astype(F32) * gain_row
    stats[0] = pack_pair(
        jnp.sum(gz, -1, keepdims=True), jnp.sum(gz * g0[:, cols(y)], -1, keepdims=True)
    )
    for dx in range(4):
        for dy in range(4):
            if dx or dy:
                put(lambda: (stats.at[0], stats.at[dx * 4 + dy],
                             dev(lax.rem(x + dx, NX), lax.rem(y + dy, NY), z, k)), ("ls", dx, dy))
    for i in range(3):
        got(lambda: out.at[:, cols(from_y[i])], ("oay", i))
    stores.append(pltpu.make_async_copy(out, out_any, lsem.at[8]))
    stores[2].start()
    for n in range(1, 16):
        got(lambda: stats.at[n], ("ls", n // 4, n % 4))
    sums_all = stats[0]
    for n in range(1, 16):
        sums_all = sums_all + stats[n]
    first, second = unpack_pair(sums_all)
    for i in range(3):
        got(lambda: gn.at[:, cols(from_y[i])], ("gay", i))
    gz = gn[...].astype(F32) * gain
    delta = rstd * (gz - first / D - g0[...] * (second / D))
    gx[...] = (cot_ref[...].astype(F32) + delta).astype(BF16)
    stores.append(pltpu.make_async_copy(gx, gx_any, lsem.at[9]))
    stores[3].start()
    w.finish()
    for store in stores:
        store.wait()
    assert len(w.sent) <= N_SEND and len(w.slots) <= N_RECV


def beside_or_far(home, diag, d, j):
    if d == 0 and j == 0:
        return jnp.logical_and(home, jnp.logical_not(diag))
    return home


def gain_cols(gain, y):
    part = gain[:, 0:PC]
    for i in range(1, NY):
        part = jnp.where(y == i, gain[:, i * PC:(i + 1) * PC], part)
    return part


def hand_kernel(a, b, c, d, ao, bo, co, do, sem):
    copies = [
        pltpu.make_async_copy(src, dst, sem.at[i])
        for i, (src, dst) in enumerate(((a, ao), (b, bo), (c, co), (d, do)))
    ]
    for copy in copies:
        copy.start()
    for copy in copies:
        copy.wait()


def per_device(inputs, cotangent, ln_gain, ln_bias, w_in, w_out):
    dma = pltpu.SemaphoreType.DMA
    tile = jax.ShapeDtypeStruct((TOK, FEAT), BF16)
    grad = jax.ShapeDtypeStruct((HIDT, FEAT), BF16)

    def vb(*shape):
        return pltpu.VMEM(shape, BF16)

    def vf(*shape):
        return pltpu.VMEM(shape, F32)

    results = pl.pallas_call(
        layer_kernel,
        name="layer",
        out_shape=[tile, tile, grad, grad],
        in_specs=[ANY] * 6,
        out_specs=[ANY] * 4,
        scratch_shapes=[
            vb(TOK, FEAT), vb(TOK, FEAT), vf(FEAT), vf(FEAT), vb(HIDT, FEAT), vb(HIDT, FEAT),
            vb(4, TOK, FEAT), vb(4, TOK, FEAT), vb(TOK, FEAT), vf(4, 8, TOK), vf(TOK, TOK),
            vf(4, HIDT, TOK), vf(2, HIDT, TOK), vb(2, HIDT, TOK), vb(2, HIDT, TOK),
            vb(3, HIDT, TOK), vb(3, HIDT, TOK), vb(HIDT, TOK), vb(2, HIDT, TOK),
            vb(4, HIDT, TOK), vb(4, HIDT, TOK), vb(4, TOK, HIDT), vb(2, HIDT, TOK),
            vb(3, TOK, FEAT), vb(3, TOK, FEAT), vf(TOK, FEAT), vb(TOK, FEAT), vb(3, TOK, PC),
            vb(TOK, PC), vb(2, NL, PR, PC), vb(2, PR, PC), vb(TOK, FEAT),
            vb(2, TOK, FEAT), vb(2, TOK, FEAT), vf(2, TOK, FEAT), vb(2, TOK, FEAT),
            vb(3, 2, TOK, PC), vb(2, TOK, PC), vb(NZ - 1, PR, PC), vf(16, 8, TOK),
            vb(TOK, FEAT), vb(TOK, FEAT), vb(HIDT, FEAT), vb(HIDT, FEAT),
            dma((N_SEND,)), dma((N_RECV,)), dma((10,)),
        ],
        compiler_params=pltpu.CompilerParams(
            collective_id=0, has_side_effects=True, vmem_limit_bytes=48 << 20
        ),
    )(inputs, cotangent, ln_gain, ln_bias, w_in.T, w_out)
    out, gx, g_in, g_out = pl.pallas_call(
        hand_kernel,
        name="hand",
        out_shape=[tile, tile, grad, grad],
        in_specs=[ANY] * 4,
        out_specs=[ANY] * 4,
        scratch_shapes=[dma((4,))],
    )(*results)
    return out, gx, g_in.T, g_out


def solution(mesh):
    return jax.shard_map(
        per_device,
        mesh=mesh,
        in_specs=(
            P("row", "col"),
            P("row", "col"),
            P("col"),
            P("col"),
            P("row", ("section", "col")),
            P(("section", "row"), "col"),
        ),
        out_specs=(
            P("row", "col"),
            P("row", "col"),
            P("row", ("section", "col")),
            P(("section", "row"), "col"),
        ),
        check_vma=False,
    )
```

time: 878 us -> 194 us (0.22)
  waiting for transfers between devices: 744 us -> 0 us
  Pallas kernels: 0 us -> 182 us
  blocking collectives: 76.2 us -> 0 us
  matrix products: 16.1 us -> 0 us
  starting transfers between devices: 16.1 us -> 0 us
  between operations: 14.2 us -> 0.67 us
    psum x1 -> x0, waiting for transfers between devices: 513 us -> none  [per_device(): branch_total = lax.psum(branch_part, 'section')]
    all_gather x4 -> x0, waiting for transfers between devices: 194 us -> none  [the longest x1 84.8 us: per_device(): lax.all_gather(w_in, 'row', axis=0, tiled=True)]
    pallas_call x0 -> x2, Pallas kernels: none -> 182 us  [the longest x1 121 us: per_device(): pl.pallas_call(layer_kernel, name='layer', out_shape=[tile, tile, grad, g...]
    all_gather x2 -> x0, blocking collectives: 56.3 us -> none  [the longest x1 43.3 us: per_device(): hid_rows = lax.all_gather(grad_hid, 'row', axis=0, tiled=True)]
    reduce_scatter x2 -> x0, waiting for transfers between devices: 22.9 us -> none  [the longest x1 22.9 us: per_device(): lax.psum_scatter(lax.dot_general(panel_rows, cotangent, (((1,), (1,)), ((...]
    psum x2 -> x0, blocking collectives: 19.8 us -> none  [the longest x1 12.4 us: per_device(): lax.psum((jnp.sum(stream_f32, -1, keepdims=True), jnp.sum(stream_f32 * st...]
    dot_general x6 -> x0, matrix products: 16.1 us -> none  [the longest x1 3.18 us: per_device(): lax.dot_general(panel_rows, cotangent, (((1,), (1,)), ((), ())), preferre...]
    all_to_all x2 -> x0, starting transfers between devices: 15.8 us -> none  [the longest x1 11.5 us: per_device(): lax.all_to_all(active_row, 'row', split_axis=1, concat_axis=0, tiled=True)]
  transfers between devices with their start and end apart: 9 -> 0, of which waited for: 7 -> 0; matrix products, arithmetic and copies ran while one was open for 2% -> 0% of each run, Pallas kernels for 0% -> 0%
where the time goes in v2:
time: 194 us; the launch traced here: 191 us
  Pallas kernels  182 us (94%)
  local copies, waits for them, and re-layouts  8.63 us (4%)
    pallas_call x1, Pallas kernels, per_device(): pl.pallas_call(layer_kernel, name='layer', out_shape=[tile, tile, grad, g...  121 us
    pallas_call x1, Pallas kernels, per_device(): pl.pallas_call(hand_kernel, name='hand', out_shape=[tile, tile, grad, gra...  60.7 us
    unnamed x20, local copies, waits for them, and re-layouts  8.63 us

profile of v2, /device:TPU:6, one launch (start us, length us, event | category | flops | bytes accessed | tf_op | source)
XLA Modules:
  0.0 191.0 jit_solution(12977572027189189945)
XLA Ops:
  0.6 0.0 copy-start
  0.6 1.1 copy-done
  1.7 0.0 copy-start.1
  1.7 1.1 copy-done.1
  2.8 0.0 copy-start.4
  2.8 1.0 copy-done.4
  3.8 0.0 copy-start.5
  3.8 1.0 copy-done.5
  4.8 0.0 copy-start.8
  4.8 0.7 copy-done.8
  5.5 0.0 copy-start.9
  5.5 0.7 copy-done.9
  6.2 121.0 %layer.1 = (bf16[128,1536]{1,0:T(8,128)(2,1)S(1)}, bf16[128,1536]{1,0:T(8,128)(2,1)S(1)}, bf16[192,1536]{1,0:T(8,128)(2,1)S(1)}, bf16[192,1536]{1,0:T(8,128)(2,1)S(1)}) custom-call(bf16[128,1536]{1,0:T(8,128)(2,1)S(1)} %copy-done.4, bf16[128,1536]{1,0:T(8,128)(2,1)S(1)} %copy-done.5, f32[1536]{0:T(1024)S(1)} %copy-done.8, f32[1536]{0:T(1024)S(1)} %copy-done.9, ...), custom_call_target="tpu_custom_call" | custom-call | tf_op jit(solution)/shard_map/layer/pallas_call | solution.py:519
  127.2 0.0 copy-start.2
  127.2 0.8 copy-done.2
  128.0 0.0 copy-start.3
  128.0 0.8 copy-done.3
  128.8 0.0 copy-start.6
  128.8 0.8 copy-done.6
  129.6 0.0 copy-start.7
  129.6 0.7 copy-done.7
  130.3 60.7 %hand.1 = (bf16[128,1536]{1,0:T(8,128)(2,1)}, bf16[128,1536]{1,0:T(8,128)(2,1)}, bf16[192,1536]{1,0:T(8,128)(2,1)}, bf16[192,1536]{1,0:T(8,128)(2,1)}) custom-call(bf16[128,1536]{1,0:T(8,128)(2,1)} %copy-done.6, bf16[128,1536]{1,0:T(8,128)(2,1)} %copy-done.7, bf16[192,1536]{1,0:T(8,128)(2,1)} %copy-done.2, bf16[192,1536]{1,0:T(8,128)(2,1)} %copy-done.3), custom_call_target="tpu_custom_call" | custom-call | tf_op jit(solution)/shard_map/hand/pallas_call | solution.py:542
Async XLA Ops:
  0.6 1.1 copy-start
  1.7 1.1 copy-start.1
  2.8 1.0 copy-start.4
  3.8 1.0 copy-start.5
  4.8 0.7 copy-start.8
  5.5 0.7 copy-start.9
  127.2 0.8 copy-start.2
  128.0 0.8 copy-start.3
  128.8 0.8 copy-start.6
  129.6 0.7 copy-start.7

commit v3 on v2

v3 whole, which is shorter than its diff:
```python
import jax
import jax.numpy as jnp
from jax import lax
from jax.experimental import pallas as pl
from jax.experimental.pallas import tpu as pltpu
from jax.sharding import PartitionSpec as P

EPS = 1e-05
SLOPE = 0.7978845608028654
CUBIC = 0.044715
F32, BF16 = jnp.float32, jnp.bfloat16
NX, NY, NZ, NL = 4, 4, 16, 8
TOK, FEAT, HIDT = 128, 1536, 192
D = NX * FEAT
QR = TOK // NY
PR, PC = TOK // NL, FEAT // NY
HBM = pl.BlockSpec(memory_space=pltpu.HBM)
NT = (((1,), (1,)), ((), ()))
TN = (((0,), (0,)), ((), ()))


def gelu_both(values):
    inner = jnp.tanh(SLOPE * (values + CUBIC * values * values * values))
    act = 0.5 * values * (1.0 + inner)
    slope = 0.5 * (1.0 + inner) + 0.5 * values * (1.0 - inner * inner) * SLOPE * (
        1.0 + 3.0 * CUBIC * values * values
    )
    return act, slope


def place():
    section, row, x = lax.axis_index("section"), lax.axis_index("row"), lax.axis_index("col")
    y, zl = lax.div(section, NL), lax.rem(section, NL)
    zh, k = lax.div(row, 2), lax.rem(row, 2)
    return x, y, zh * NL + zl, zh, zl, k, row


def dev(x, y, z, k):
    return (y * NL + lax.rem(z, NL), lax.div(z, NL) * 2 + k, x)

def al(value, mult):
    return pl.multiple_of(value, mult)


def pack_pair(first, second):
    lane = lax.broadcasted_iota(jnp.int32, (TOK, TOK), 1)
    both = jnp.where(lane == 0, first, jnp.where(lane == 1, second, 0.0))
    return both.T[0:8, :]


def unpack_pair(packed):
    both = jnp.concatenate([packed, jnp.zeros((TOK - 8, TOK), F32)], axis=0).T
    return both[:, 0:1], both[:, 1:2]


def arrived(ref, sem):
    pltpu.make_async_copy(ref, ref, sem).wait()


class Wires:
    def __init__(self, ssem, rsem):
        self.ssem, self.rsem = ssem, rsem
        self.slots, self.sent = {}, []

    def slot(self, *name):
        return self.rsem.at[self.slots.setdefault(name, len(self.slots))]

    def block(self, name, size):
        base = len(self.slots)
        for i in range(size):
            self.slot(name, i)
        return lambda i: self.rsem.at[base + i]

    def put(self, make, name, pred=None):
        rsem = self.slot(*name) if isinstance(name, tuple) else name
        ssem = self.ssem.at[len(self.sent)]

        src, dst, to = make()

        def copy():
            return pltpu.make_async_remote_copy(
                src_ref=src, dst_ref=dst, send_sem=ssem, recv_sem=rsem,
                device_id=to, device_id_type=pl.DeviceIdType.MESH,
            )

        when(pred, lambda: copy().start())
        self.sent.append((pred, copy))

    def got(self, make, name, pred=None):
        ref = make()
        sem = self.slot(*name) if isinstance(name, tuple) else name
        when(pred, lambda: arrived(ref, sem))

    def finish(self):
        for pred, copy in self.sent:
            when(pred, lambda copy=copy: copy().wait_send())


def when(pred, act):
    if pred is None:
        act()
    else:
        pl.when(pred)(act)


def both(*flags):
    result = flags[0]
    for flag in flags[1:]:
        result = jnp.logical_and(result, flag)
    return result


N_SEND, N_RECV = 190, 160


def layer_kernel(
    x_any, cot_any, gain_any, bias_any, win_any, wout_any,
    out_any, gx_any, gin_any, gout_any,
    x_ref, cot_ref, gain_ref, bias_ref, w_in, w_out,
    X, C, xn, sums, st_ref,
    hs, hr, us, ur, qs, qr, ts, tr, aT, at,
    WX, gA, g0, gq, g1r, g2, g2r, gp, gn, sc, stb,
    os, orr, o0, o1, o1r, o2, o2r, stats, out, gx, g_in, g_out,
    ssem, rsem, lsem,
):
    x, y, z, zh, zl, k, r = place()
    no = jnp.logical_not
    w = Wires(ssem, rsem)
    put, got = w.put, w.got
    loads = [
        pltpu.make_async_copy(src, dst, lsem.at[i])
        for i, (src, dst) in enumerate((
            (x_any, x_ref), (cot_any, cot_ref), (gain_any, gain_ref),
            (bias_any, bias_ref), (win_any, w_in), (wout_any, w_out),
        ))
    ]
    for load in loads:
        load.start()
    zm, zp = NZ - 1 - z, (1 - zh) * NL + zl
    par = lax.rem(zl, 2)
    zn = z + 1 - 2 * par
    xs = [lax.rem(x + d, NX) for d in (1, 2, 3)]
    ys = [lax.rem(y + d, NY) for d in (1, 2, 3)]
    zs = [lax.rem(z + d, NZ) for d in range(1, NZ)]
    ls = [lax.rem(zl + d, NL) for d in range(NL)]
    diag = r == x
    zb, kb = lax.div(x, 2), lax.rem(x, 2)
    home = zb == zh
    beside = jnp.logical_and(home, k != kb)
    core, pair = dev(x, y, z, 1 - k), dev(x, y, zp, k)
    zr, kt, ze = lax.div(zl, 4), lax.rem(lax.div(zl, 2), 2), lax.rem(zl, 2)
    owns = both(zr == zb, kt == k, k == kb)

    barrier = pltpu.get_barrier_semaphore()

    def greet(peer, pred=None):
        when(pred, lambda: pl.semaphore_signal(
            barrier, inc=1, device_id=peer, device_id_type=pl.DeviceIdType.MESH))

    for p in zs:
        greet(dev(x, y, p, k))
    greet(core)
    greet(dev(x, y, zm, 1 - k))
    for dx in range(4):
        for dy in range(4):
            if dx or dy:
                greet(dev(lax.rem(x + dx, NX), lax.rem(y + dy, NY), z, k))
    section = lax.axis_index("section")
    for half in range(2):
        greet((section, x, half * 2 + k), no(jnp.logical_and(diag, zh == half)))
    greet(dev(r, y, z, 1 - k), no(diag))
    for q in range(NX):
        for e in range(2):
            greet(dev(q, y, zh * NL + zb * 4 + k * 2 + e, kb),
                  no(both(owns, x == q, lax.rem(zl, 2) == e)))

    def num(flag):
        return flag.astype(jnp.int32)
    total = 15 + 2 + 15 + 2 - num(diag) + 3 * num(beside) + 8 - num(owns)

    loads[0].wait()
    rows = x_ref[...].astype(F32)
    sums[0] = pack_pair(
        jnp.sum(rows, -1, keepdims=True), jnp.sum(rows * rows, -1, keepdims=True)
    )
    loads[1].wait()
    loads[2].wait()
    loads[3].wait()
    pl.semaphore_wait(barrier, total)

    def rows_at(start, size):
        return pl.ds(al(start, 16), size)

    def cols(p):
        return pl.ds(al(p * PC, PC), PC)

    def prow(p):
        return pl.ds(al(p * PR, PR), PR)

    mine8 = rows_at(y * QR + par * 16, 16)
    theirs8 = rows_at(y * QR + (1 - par) * 16, 16)
    quarter = rows_at(y * QR, QR)
    front, back = (slice(None), pl.ds(0, PC)), (quarter, pl.ds(PC, FEAT - PC))
    tiles = [zh * 2 + k, zh * 2 + 1 - k, (1 - zh) * 2 + k, (1 - zh) * 2 + 1 - k]

    for i, p in enumerate(xs):
        put(lambda: (sums.at[0], sums.at[1 + i], dev(p, y, z, k)), ("stat", i))
    loads[4].wait()
    for i in (1, 0, 2):
        put(lambda: (w_in.at[:, cols(xs[i])], WX.at[x], dev(xs[i], y, z, k)), ("wx", i))
    WX[x] = w_in[:, cols(x)]
    put(lambda: (cot_ref.at[mine8], C.at[r, mine8], dev(x, y, zm, k)), ("cz",))
    put(lambda: (cot_ref, C.at[r], core), ("cc",))
    C[r] = cot_ref[...]
    for i in range(3):
        got(lambda: sums.at[1 + i], ("stat", i))
    first, second = unpack_pair((sums[0] + sums[1]) + (sums[2] + sums[3]))
    mean = first / D
    rstd = lax.rsqrt(second / D - mean * mean + EPS)
    lane = lax.broadcasted_iota(jnp.int32, (TOK, TOK), 1)
    st_ref[...] = jnp.where(lane == 0, mean, rstd)
    gain = gain_ref[...].reshape(1, FEAT)
    bias = bias_ref[...].reshape(1, FEAT)
    xn[...] = ((x_ref[...].astype(F32) - mean) * rstd * gain + bias).astype(BF16)

    away = no(home)
    for j in range(2):
        put(lambda: (xn.at[mine8], X.at[r, mine8], dev(x, y, zm, k if j == 0 else 1 - k)),
            ("xz", j), jnp.logical_and(away, (k == kb) if j == 0 else (k != kb)))
    put(lambda: (xn.at[back], X.at[(r, *back)], core), ("xb", 1), beside)
    put(lambda: (xn.at[front], X.at[(r, *front)], core), ("xf", 1), beside)

    @pl.when(diag)
    def _():
        X[(r, *back)] = xn[back]
        X[(r, *front)] = xn[front]

    def spread(ref, name):
        for i, p in enumerate(xs):
            put(lambda: (ref, ref, dev(p, y, z, k)), name, diag)

    def along_y(ref, name):
        for i, p in enumerate(ys):
            put(lambda: (ref, ref, dev(x, p, z, k)), name + (i,))

    for d in range(2):
        ref = X.at[(tiles[d], *back)]
        got(lambda: ref, ("xb", d), no(diag) if d == 0 else None)
        spread(ref, ("xb", d))
        along_y(ref, ("yb", d))
    spread(X.at[(tiles[0], *front)], ("xf", 0))
    got(lambda: X.at[(tiles[1], *front)], ("xf", 1), diag)
    spread(X.at[(tiles[1], *front)], ("xf", 1))
    got(lambda: C.at[tiles[2], theirs8], ("cz",))
    put(lambda: (C.at[tiles[2], theirs8], C.at[tiles[2], theirs8], dev(x, y, zn, k)), ("cn",))
    for d in (2, 3):
        ref = X.at[tiles[d], theirs8]
        got(lambda: ref, ("xz", d - 2), diag)
        put(lambda: (ref, ref, dev(x, y, zn, k)), ("xn", d), diag)
    got(lambda: C.at[tiles[2], mine8], ("cn",))
    along_y(C.at[tiles[2], quarter], ("cy",))
    for d in (2, 3):
        got(lambda: X.at[tiles[d], mine8], ("xn", d), diag)
        spread(X.at[tiles[d], quarter], ("xq", d))
    for d in (2, 3):
        ref = X.at[tiles[d], quarter]
        got(lambda: ref, ("xq", d), no(diag))
        along_y(ref, ("yq", d))
    from_y = [lax.rem(y + NY - 1 - i, NY) for i in range(3)]
    from_x = [lax.rem(x + NX - 1 - i, NX) for i in range(3)]

    loads[5].wait()
    for d in range(2):
        got(lambda: X.at[(tiles[d], *front)], ("xf", d), no(diag))
        for i in range(3):
            got(lambda: X.at[tiles[d], rows_at(from_y[i] * QR, QR), pl.ds(PC, FEAT - PC)], ("yb", d, i))

    def hid(t):
        return lax.dot_general(w_in[...], X[t], NT, preferred_element_type=F32)

    def grad(t):
        return lax.dot_general(w_out[...], C[t], NT, preferred_element_type=F32)

    hs[0] = hid(tiles[1])
    put(lambda: (hs.at[0], hr.at[0], core), ("hc", 0))
    near = hid(tiles[0])
    for i in range(3):
        got(lambda: C.at[tiles[2], rows_at(from_y[i] * QR, QR)], ("cy", i))
    put(lambda: (C.at[tiles[2]], C.at[tiles[2]], core), ("cf",))
    got(lambda: hr.at[0], ("hc", 0))
    h_near = near + hr[0]
    us[0] = h_near.astype(BF16)
    put(lambda: (us.at[0], ur.at[1], pair), ("hz", 0))
    hs[2] = h_near
    got(lambda: C.at[tiles[1]], ("cc",))
    got(lambda: C.at[tiles[3]], ("cf",))
    for i in (1, 0, 2):
        qs[i] = grad(xs[i]).astype(BF16)
        put(lambda: (qs.at[i], qr.at[i], dev(xs[i], y, z, k)), ("ga", i))
    own = grad(x)
    for i in range(3):
        got(lambda: qr.at[i], ("ga", i))
    ts[...] = (own + qr[0].astype(F32) + qr[1].astype(F32) + qr[2].astype(F32)).astype(BF16)
    for half in range(2):
        selfish = jnp.logical_and(diag, zh == half)
        for side in range(2):
            put(lambda: (ts, tr.at[side], (section, half * 2 + kb, r)), ("gt", side),
                jnp.logical_and(no(selfish), zb == side))

    @pl.when(diag)
    def _():
        tr[zh] = ts[...]

    for d in (2, 3):
        for i in range(3):
            got(lambda: X.at[tiles[d], rows_at(from_y[i] * QR, QR)], ("yq", d, i))
    hs[1] = hid(tiles[3])
    put(lambda: (hs.at[1], hr.at[1], core), ("hc", 1))
    far = hid(tiles[2])
    got(lambda: hr.at[1], ("hc", 1))
    h_far = far + hr[1]
    us[1] = h_far.astype(BF16)
    put(lambda: (us.at[1], ur.at[0], pair), ("hz", 1))
    hs[3] = h_far
    for side in range(2):
        got(lambda: tr.at[side], ("gt", side), no(jnp.logical_and(diag, zh == side)))

    def activate(step, half):
        act, slope = gelu_both(hs[2 + step] + ur[step].astype(F32))
        gA[k * 2 + half, x] = (tr[half].astype(F32) * slope).astype(BF16)
        at[half] = act.astype(BF16)

    def spread_gh(step, pos):
        ref = gA.at[pos, x]
        for i in (1, 0, 2):
            put(lambda: (ref, ref, dev(xs[i], y, z, k)), ("gg", step, i))
        put(lambda: (ref, ref, core), ("gc", step))

    got(lambda: ur.at[1], ("hz", 0))
    activate(1, 1 - zh)
    spread_gh(1, k * 2 + 1 - zh)
    got(lambda: ur.at[0], ("hz", 1))
    activate(0, zh)
    spread_gh(0, k * 2 + zh)
    held = pl.ds(k * 2, 2)
    for i, p in enumerate(xs):
        put(lambda: (at, aT.at[held], dev(p, y, z, k)), ("ax", 0), diag)
    for i, p in enumerate(xs):
        put(lambda: (at, aT.at[held], dev(p, y, z, 1 - k)), ("ax", 1), beside)
    put(lambda: (at, aT.at[held], core), ("ax", 1), beside)

    @pl.when(diag)
    def _():
        aT[held] = at[...]

    unheld = pl.ds((1 - k) * 2, 2)
    for i in (0, 2, 1):
        for step, pos in ((1, k * 2 + 1 - zh), (0, k * 2 + zh)):
            got(lambda: gA.at[pos, from_x[i]], ("gg", step, i))
        put(lambda: (gA.at[held, from_x[i]], gA.at[held, from_x[i]], core), ("gf", i))
    for i in range(3):
        got(lambda: WX.at[from_x[i]], ("wx", i))
    got(lambda: gA.at[(1 - k) * 2 + 1 - zh, x], ("gc", 1))
    got(lambda: gA.at[(1 - k) * 2 + zh, x], ("gc", 0))
    for i in (0, 2, 1):
        got(lambda: gA.at[unheld, from_x[i]], ("gf", i))

    slab = WX[...].reshape(NX * HIDT, PC)
    for p in range(4):
        g0[p] = lax.dot_general(
            gA[p].reshape(NX * HIDT, TOK), slab, TN, preferred_element_type=F32)
    gq[...] = g0[...].astype(BF16)
    for i in (1, 0, 2):
        put(lambda: (gq.at[:, rows_at(ys[i] * QR, QR)], g1r.at[i], dev(x, ys[i], z, k)), ("gy", i))

    got(lambda: aT.at[held], ("ax", 0), no(diag))
    got(lambda: aT.at[unheld], ("ax", 1))
    halves = (1 - zh, zh)

    def part_o(pos):
        return lax.dot_general(aT[pos], w_out[...], TN, preferred_element_type=F32)

    for c in range(2):
        os[c] = part_o((1 - k) * 2 + halves[c]).astype(BF16)
        put(lambda: (os.at[c], orr.at[c], core), ("oc", c))
    for c in range(2):
        o0[c] = part_o(k * 2 + halves[c])
    for c in range(2):
        got(lambda: orr.at[c], ("oc", c))
        o1[c] = (o0[c] + orr[c].astype(F32)).astype(BF16)
        for i in (1, 0, 2):
            put(lambda: (o1.at[c, :, cols(ys[i])], o1r.at[c, i], dev(x, ys[i], z, k)), ("oy", c, i))

    def weight_grad(left, right):
        acc = jnp.dot(left(0), right[0], preferred_element_type=F32)
        for t in range(1, 4):
            acc = acc + jnp.dot(left((t % 2) * 2 + t // 2), right[t], preferred_element_type=F32)
        return acc.astype(BF16)

    g_out[...] = weight_grad(lambda p: aT[p], C)
    stores = [pltpu.make_async_copy(g_out, gout_any, lsem.at[6])]
    stores[0].start()

    for i in range(3):
        got(lambda: g1r.at[i], ("gy", i))
    g2[...] = (
        g0[:, quarter, :] + g1r[0].astype(F32) + g1r[1].astype(F32) + g1r[2].astype(F32)
    ).astype(BF16)
    zsem = w.block("gz", NL)
    for p in range(4):
        for e in range(2):
            target = (p % 2) * NL + zh * 4 + (p // 2) * 2 + e
            put(lambda: (g2.at[p, pl.ds(e * 16, 16)], g2r.at[zl], dev(x, y, target, k)),
                zsem(zl), z != target)
    mine_here = zr == zh

    @pl.when(mine_here)
    def _():
        g2r[zl] = g2[kt * 2 + zh, rows_at(ze * 16, 16), :]

    g_in[...] = weight_grad(lambda p: gA[p, x], X)
    stores.append(pltpu.make_async_copy(g_in, gin_any, lsem.at[7]))
    stores[1].start()

    for c in range(2):
        for i in range(3):
            got(lambda: o1r.at[c, i], ("oy", c, i))
        o2[c] = (
            o1[c, :, cols(y)].astype(F32) + o1r[c, 0].astype(F32)
            + o1r[c, 1].astype(F32) + o1r[c, 2].astype(F32)
        ).astype(BF16)
        for d in range(c, NL):
            target = halves[c] * NL + ls[d]
            put(lambda: (o2.at[c, prow(ls[d])], o2r.at[c, d], dev(x, y, target, k)), ("oz", c, d))

    for n in range(NL):
        got(lambda: g2r.at[n], zsem(n), no(both(mine_here, zl == n)))
    piece = g2r[0].astype(F32)
    for n in range(1, NL):
        piece = piece + g2r[n].astype(F32)
    gp[...] = piece.astype(BF16)
    asem = w.block("gal", NX * 2)
    here = (rows_at(y * QR + ze * 16, 16), cols(x))
    for d in range(NL):
        put(lambda: (gp, gn.at[here], dev(zr * 2 + k, y, zh * NL + ls[d], kt)),
            asem(x * 2 + ze), no(owns) if d == 0 else None)

    @pl.when(owns)
    def _():
        gn[here] = gp[...]

    mine = (prow(zl), cols(y))
    for c in range(2):
        for d in range(c, NL):
            got(lambda: o2r.at[c, d], ("oz", c, d))
    piece = o2[1, prow(zl), :].astype(F32)
    for c in range(2):
        for d in range(c, NL):
            piece = piece + o2r[c, d].astype(F32)
    out[mine] = (x_ref[mine].astype(F32) + piece).astype(BF16)
    for d in range(1, NL):
        put(lambda: (out.at[mine], out.at[mine], dev(x, y, zh * NL + ls[d], k)), ("oal", d))

    mean, rstd = st_ref[:, 0:1], st_ref[:, 1:2]
    sc[...] = (x_ref[...].astype(F32) - mean) * rstd
    stb[...] = jnp.zeros((TOK, TOK), F32)
    for q in range(NX):
        for e in range(2):
            got(lambda: gn.at[rows_at(y * QR + e * 16, 16), pl.ds(q * PC, PC)], asem(q * 2 + e),
                no(both(owns, x == q, ze == e)))
    for i in (1, 0, 2):
        put(lambda: (gn.at[quarter], gn.at[quarter], dev(x, ys[i], z, k)), ("gay", i))
    gz = gn[quarter, :].astype(F32) * gain
    lane = lax.broadcasted_iota(jnp.int32, (QR, TOK), 1)
    first = jnp.sum(gz, -1, keepdims=True)
    second = jnp.sum(gz * sc[quarter, :], -1, keepdims=True)
    stb[quarter, :] = jnp.where(lane == 0, first, jnp.where(lane == 1, second, 0.0))
    stats[0] = stb[...].T[0:8, :]
    for dx in range(4):
        for dy in range(4):
            if dx or dy:
                put(lambda: (stats.at[0], stats.at[dx * 4 + dy],
                             dev(lax.rem(x + dx, NX), lax.rem(y + dy, NY), z, k)), ("ls", dx, dy))
    from_l = [lax.rem(zl + NL - d, NL) for d in range(NL)]
    for d in range(1, NL):
        got(lambda: out.at[prow(from_l[d]), cols(y)], ("oal", d))
    for i in (1, 0, 2):
        put(lambda: (out.at[:, cols(y)], out.at[:, cols(y)], dev(x, ys[i], z, k)), ("oay", i))
    for n in range(1, 16):
        got(lambda: stats.at[n], ("ls", n // 4, n % 4))
    sums_all = stats[0]
    for n in range(1, 16):
        sums_all = sums_all + stats[n]
    first, second = unpack_pair(sums_all)
    for i in range(3):
        got(lambda: gn.at[rows_at(from_y[i] * QR, QR)], ("gay", i))
    gz = gn[...].astype(F32) * gain
    delta = rstd * (gz - first / D - sc[...] * (second / D))
    gx[...] = (cot_ref[...].astype(F32) + delta).astype(BF16)
    stores.append(pltpu.make_async_copy(gx, gx_any, lsem.at[9]))
    stores[2].start()
    for i in range(3):
        got(lambda: out.at[:, cols(from_y[i])], ("oay", i))
    stores.append(pltpu.make_async_copy(out, out_any, lsem.at[8]))
    stores[3].start()
    w.finish()
    for store in stores:
        store.wait()
    assert len(w.sent) <= N_SEND and len(w.slots) <= N_RECV


def per_device(inputs, cotangent, ln_gain, ln_bias, w_in, w_out):
    dma = pltpu.SemaphoreType.DMA
    tile = jax.ShapeDtypeStruct((TOK, FEAT), BF16)
    grad = jax.ShapeDtypeStruct((HIDT, FEAT), BF16)

    def vb(*shape):
        return pltpu.VMEM(shape, BF16)

    def vf(*shape):
        return pltpu.VMEM(shape, F32)

    out, gx, g_in, g_out = pl.pallas_call(
        layer_kernel,
        name="layer",
        out_shape=[tile, tile, grad, grad],
        in_specs=[HBM] * 6,
        out_specs=[HBM] * 4,
        scratch_shapes=[
            vb(TOK, FEAT), vb(TOK, FEAT), vf(FEAT), vf(FEAT), vb(HIDT, FEAT), vb(HIDT, FEAT),
            vb(4, TOK, FEAT), vb(4, TOK, FEAT), vb(TOK, FEAT), vf(4, 8, TOK), vf(TOK, TOK),
            vf(4, HIDT, TOK), vf(2, HIDT, TOK), vb(2, HIDT, TOK), vb(2, HIDT, TOK),
            vb(3, HIDT, TOK), vb(3, HIDT, TOK), vb(HIDT, TOK), vb(2, HIDT, TOK),
            vb(4, HIDT, TOK), vb(2, HIDT, TOK),
            vb(NX, HIDT, PC), vb(4, NX, HIDT, TOK), vf(4, TOK, PC), vb(4, TOK, PC), vb(3, 4, QR, PC),
            vb(4, QR, PC), vb(NL, PR, PC), vb(PR, PC), vb(TOK, FEAT), vf(TOK, FEAT), vf(TOK, TOK),
            vb(2, TOK, FEAT), vb(2, TOK, FEAT), vf(2, TOK, FEAT), vb(2, TOK, FEAT),
            vb(2, 3, TOK, PC), vb(2, TOK, PC), vb(2, NL, PR, PC), vf(16, 8, TOK),
            vb(TOK, FEAT), vb(TOK, FEAT), vb(HIDT, FEAT), vb(HIDT, FEAT),
            dma((N_SEND,)), dma((N_RECV,)), dma((10,)),
        ],
        compiler_params=pltpu.CompilerParams(
            collective_id=0, has_side_effects=True, vmem_limit_bytes=63 << 20
        ),
    )(inputs, cotangent, ln_gain, ln_bias, w_in.T, w_out)
    return out, gx, g_in.T, g_out


def solution(mesh):
    return jax.shard_map(
        per_device,
        mesh=mesh,
        in_specs=(
            P("row", "col"),
            P("row", "col"),
            P("col"),
            P("col"),
            P("row", ("section", "col")),
            P(("section", "row"), "col"),
        ),
        out_specs=(
            P("row", "col"),
            P("row", "col"),
            P("row", ("section", "col")),
            P(("section", "row"), "col"),
        ),
        check_vma=False,
    )
```

time: 194 us -> 116 us (0.60)
  Pallas kernels: 182 us -> 109 us
  local copies, waits for them, and re-layouts: 8.63 us -> 4.69 us
    pallas_call x1 -> x0, Pallas kernels: 60.7 us -> none  [per_device(): pl.pallas_call(hand_kernel, name='hand', out_shape=[tile, tile, grad, gra...]
    pallas_call x1, Pallas kernels: 121 us -> 109 us  [per_device(): pl.pallas_call(layer_kernel, name='layer', out_shape=[tile, tile, grad, g...]
    unnamed x20 -> x10, local copies, waits for them, and re-layouts: 8.63 us -> 4.69 us
where the time goes in v3:
time: 116 us; the launch traced here: 115 us
  Pallas kernels  109 us (94%)
  local copies, waits for them, and re-layouts  4.69 us (4%)
    pallas_call x1, Pallas kernels, per_device(): pl.pallas_call(layer_kernel, name='layer', out_shape=[tile, tile, grad, g...  109 us
    unnamed x10, local copies, waits for them, and re-layouts  4.69 us

profile of v3, /device:TPU:6, one launch (start us, length us, event | category | flops | bytes accessed | tf_op | source)
XLA Modules:
  0.0 114.5 jit_solution(13640616826439809445)
XLA Ops:
  0.6 109.2 %layer.1 = (bf16[128,1536]{1,0:T(8,128)(2,1)}, bf16[128,1536]{1,0:T(8,128)(2,1)}, bf16[192,1536]{1,0:T(8,128)(2,1)}, bf16[192,1536]{1,0:T(8,128)(2,1)}) custom-call(bf16[128,1536]{1,0:T(8,128)(2,1)} %x_any.1, bf16[128,1536]{1,0:T(8,128)(2,1)} %cot_any.1, f32[1536]{0:T(1024)} %gain_any.1, f32[1536]{0:T(1024)} %bias_any.1, bf16[192,1536]{1,0:T(8,128)(2,1)} %bitcast.3, ...), custom_call_target="tpu_custom_call" | custom-call | tf_op jit(solution)/shard_map/layer/pallas_call | solution.py:523
  109.8 0.0 copy-start.2
  109.8 0.0 copy-start.1
  109.9 1.8 %copy.14 = bf16[128,1536]{1,0:T(8,128)(2,1)} copy(bf16[128,1536]{1,0:T(8,128)(2,1)} %get-tuple-element.16) | data formatting | bytes 786432
  111.7 0.0 copy-done.2
  111.7 0.7 copy.15
  112.4 0.0 copy-done.1
  112.5 0.0 copy-start
  112.5 0.8 copy.16
  113.3 0.5 copy-done
  113.7 0.8 copy.17
Async XLA Ops:
  109.8 1.9 %copy-start.2 = (bf16[128,1536]{1,0:T(8,128)(2,1)S(1)}, bf16[128,1536]{1,0:T(8,128)(2,1)}, u32[]{:S(2)}) copy-start(bf16[128,1536]{1,0:T(8,128)(2,1)} %get-tuple-element.17) | copy-start | bytes 1179652
  109.8 2.6 %copy-start.1 = (bf16[192,1536]{1,0:T(8,128)(2,1)S(1)}, bf16[192,1536]{1,0:T(8,128)(2,1)}, u32[]{:S(2)}) copy-start(bf16[192,1536]{1,0:T(8,128)(2,1)} %get-tuple-element.10) | copy-start | bytes 1769476
  112.5 1.3 %copy-start = (bf16[192,1536]{1,0:T(8,128)(2,1)S(1)}, bf16[192,1536]{1,0:T(8,128)(2,1)}, u32[]{:S(2)}) copy-start(bf16[192,1536]{1,0:T(8,128)(2,1)} %get-tuple-element.19) | copy-start | bytes 1769476

commit v4 on v3

--- a/solution.py
+++ b/solution.py
@@ -14,6 +14,7 @@
 D = NX * FEAT
 QR = TOK // NY
 PR, PC = TOK // NL, FEAT // NY
+VMEM = pl.BlockSpec(memory_space=pltpu.VMEM)
 HBM = pl.BlockSpec(memory_space=pltpu.HBM)
 NT = (((1,), (1,)), ((), ()))
 TN = (((0,), (0,)), ((), ()))
@@ -117,7 +118,7 @@
     x_any, cot_any, gain_any, bias_any, win_any, wout_any,
     out_any, gx_any, gin_any, gout_any,
     x_ref, cot_ref, gain_ref, bias_ref, w_in, w_out,
-    X, C, xn, sums, st_ref,
+    X, C, N, sums, pairs, gb, st_ref,
     hs, hr, us, ur, qs, qr, ts, tr, aT, at,
     WX, gA, g0, gq, g1r, g2, g2r, gp, gn, sc, stb,
     os, orr, o0, o1, o1r, o2, o2r, stats, out, gx, g_in, g_out,
@@ -203,80 +204,119 @@
     front, back = (slice(None), pl.ds(0, PC)), (quarter, pl.ds(PC, FEAT - PC))
     tiles = [zh * 2 + k, zh * 2 + 1 - k, (1 - zh) * 2 + k, (1 - zh) * 2 + 1 - k]
 
+    def spread_x(ref, name):
+        for i in (1, 0, 2):
+            put(lambda: (ref, ref, dev(xs[i], y, z, k)), name, diag)
+
+    def along_y(ref, name):
+        for i in (1, 0, 2):
+            put(lambda: (ref, ref, dev(x, ys[i], z, k)), name + (i,))
+
+    from_y = [lax.rem(y + NY - 1 - i, NY) for i in range(3)]
+    from_x = [lax.rem(x + NX - 1 - i, NX) for i in range(3)]
+    away = no(home)
+
     for i, p in enumerate(xs):
         put(lambda: (sums.at[0], sums.at[1 + i], dev(p, y, z, k)), ("stat", i))
+    for j in range(2):
+        put(lambda: (x_ref.at[mine8], X.at[r, mine8], dev(x, y, zm, k if j == 0 else 1 - k)),
+            ("xz", j), jnp.logical_and(away, (k == kb) if j == 0 else (k != kb)))
+    put(lambda: (x_ref.at[back], X.at[(r, *back)], core), ("xb", 1), beside)
+    put(lambda: (x_ref.at[front], X.at[(r, *front)], core), ("xf", 1), beside)
+    put(lambda: (cot_ref, C.at[r], core), ("cc",))
+
+    @pl.when(diag)
+    def _():
+        X[(r, *back)] = x_ref[back]
+        X[(r, *front)] = x_ref[front]
+
+    for d in range(2):
+        ref = X.at[(tiles[d], *back)]
+        if d:
+            got(lambda: ref, ("xb", d), diag)
+        spread_x(ref, ("xb", d))
+    gain = gain_ref[...].reshape(1, FEAT)
+    bias = bias_ref[...].reshape(1, FEAT)
+
+    @pl.when(diag)
+    def _():
+        gb[0:1, :] = gain
+        gb[1:2, :] = bias
+
+    spread_x(gb, ("gb",))
+    spread_x(X.at[(tiles[0], *front)], ("xf", 0))
+    got(lambda: X.at[(tiles[1], *front)], ("xf", 1), diag)
+    spread_x(X.at[(tiles[1], *front)], ("xf", 1))
+    C[r] = cot_ref[...]
+    for i in range(3):
+        got(lambda: sums.at[1 + i], ("stat", i))
+    pairs[0] = (sums[0] + sums[1]) + (sums[2] + sums[3])
+    for d, to in ((2, dev(x, y, zm, k)), (3, dev(x, y, zm, 1 - k)), (1, core)):
+        put(lambda: (pairs.at[0], pairs.at[d], to), ("pair", d))
+    put(lambda: (cot_ref.at[mine8], C.at[r, mine8], dev(x, y, zm, k)), ("cz",))
+
+    def moments(d):
+        first, second = unpack_pair(pairs[d])
+        mean = first / D
+        return mean, lax.rsqrt(second / D - mean * mean + EPS)
+
+    mean, rstd = moments(0)
+    lane = lax.broadcasted_iota(jnp.int32, (TOK, TOK), 1)
+    st_ref[...] = jnp.where(lane == 0, mean, rstd)
+    for d in range(2):
+        ref = X.at[(tiles[d], *back)]
+        got(lambda: ref, ("xb", d), no(diag))
+        along_y(ref, ("yb", d))
+    two, three = X.at[tiles[2], theirs8], X.at[tiles[3], theirs8]
+    got(lambda: two, ("xz", 0), diag)
+    put(lambda: (two, two, dev(x, y, zn, k)), ("xn",), diag)
+    got(lambda: three, ("xz", 1), diag)
+    spread_x(three, ("xe",))
+    got(lambda: X.at[tiles[2], mine8], ("xn",), diag)
+    spread_x(X.at[tiles[2], quarter], ("xq",))
+    got(lambda: C.at[tiles[2], theirs8], ("cz",))
+    other = C.at[tiles[2], theirs8]
+    along_y(other, ("cy",))
+    put(lambda: (other, other, dev(x, y, zn, k)), ("ce", 3))
+    got(lambda: three, ("xe",), no(diag))
+    along_y(three, ("ye",))
+    put(lambda: (three, three, dev(x, y, zn, k)), ("ze", 3))
+    got(lambda: X.at[tiles[2], quarter], ("xq",), no(diag))
+    along_y(X.at[tiles[2], quarter], ("yq",))
     loads[4].wait()
     for i in (1, 0, 2):
         put(lambda: (w_in.at[:, cols(xs[i])], WX.at[x], dev(xs[i], y, z, k)), ("wx", i))
     WX[x] = w_in[:, cols(x)]
-    put(lambda: (cot_ref.at[mine8], C.at[r, mine8], dev(x, y, zm, k)), ("cz",))
-    put(lambda: (cot_ref, C.at[r], core), ("cc",))
-    C[r] = cot_ref[...]
-    for i in range(3):
-        got(lambda: sums.at[1 + i], ("stat", i))
-    first, second = unpack_pair((sums[0] + sums[1]) + (sums[2] + sums[3]))
-    mean = first / D
-    rstd = lax.rsqrt(second / D - mean * mean + EPS)
-    lane = lax.broadcasted_iota(jnp.int32, (TOK, TOK), 1)
-    st_ref[...] = jnp.where(lane == 0, mean, rstd)
-    gain = gain_ref[...].reshape(1, FEAT)
-    bias = bias_ref[...].reshape(1, FEAT)
-    xn[...] = ((x_ref[...].astype(F32) - mean) * rstd * gain + bias).astype(BF16)
-
-    away = no(home)
-    for j in range(2):
-        put(lambda: (xn.at[mine8], X.at[r, mine8], dev(x, y, zm, k if j == 0 else 1 - k)),
-            ("xz", j), jnp.logical_and(away, (k == kb) if j == 0 else (k != kb)))
-    put(lambda: (xn.at[back], X.at[(r, *back)], core), ("xb", 1), beside)
-    put(lambda: (xn.at[front], X.at[(r, *front)], core), ("xf", 1), beside)
-
-    @pl.when(diag)
-    def _():
-        X[(r, *back)] = xn[back]
-        X[(r, *front)] = xn[front]
-
-    def spread(ref, name):
-        for i, p in enumerate(xs):
-            put(lambda: (ref, ref, dev(p, y, z, k)), name, diag)
-
-    def along_y(ref, name):
-        for i, p in enumerate(ys):
-            put(lambda: (ref, ref, dev(x, p, z, k)), name + (i,))
-
-    for d in range(2):
-        ref = X.at[(tiles[d], *back)]
-        got(lambda: ref, ("xb", d), no(diag) if d == 0 else None)
-        spread(ref, ("xb", d))
-        along_y(ref, ("yb", d))
-    spread(X.at[(tiles[0], *front)], ("xf", 0))
-    got(lambda: X.at[(tiles[1], *front)], ("xf", 1), diag)
-    spread(X.at[(tiles[1], *front)], ("xf", 1))
-    got(lambda: C.at[tiles[2], theirs8], ("cz",))
-    put(lambda: (C.at[tiles[2], theirs8], C.at[tiles[2], theirs8], dev(x, y, zn, k)), ("cn",))
-    for d in (2, 3):
-        ref = X.at[tiles[d], theirs8]
-        got(lambda: ref, ("xz", d - 2), diag)
-        put(lambda: (ref, ref, dev(x, y, zn, k)), ("xn", d), diag)
-    got(lambda: C.at[tiles[2], mine8], ("cn",))
-    along_y(C.at[tiles[2], quarter], ("cy",))
-    for d in (2, 3):
-        got(lambda: X.at[tiles[d], mine8], ("xn", d), diag)
-        spread(X.at[tiles[d], quarter], ("xq", d))
-    for d in (2, 3):
-        ref = X.at[tiles[d], quarter]
-        got(lambda: ref, ("xq", d), no(diag))
-        along_y(ref, ("yq", d))
-    from_y = [lax.rem(y + NY - 1 - i, NY) for i in range(3)]
-    from_x = [lax.rem(x + NX - 1 - i, NX) for i in range(3)]
+    got(lambda: gb, ("gb",), no(diag))
+
+    def normalize(d):
+        if d:
+            got(lambda: pairs.at[d], ("pair", d))
+        mean, rstd = moments(d)
+        N[tiles[d]] = (
+            (X[tiles[d]].astype(F32) - mean) * rstd * gb[0:1, :] + gb[1:2, :]
+        ).astype(BF16)
 
     loads[5].wait()
     for d in range(2):
         got(lambda: X.at[(tiles[d], *front)], ("xf", d), no(diag))
         for i in range(3):
             got(lambda: X.at[tiles[d], rows_at(from_y[i] * QR, QR), pl.ds(PC, FEAT - PC)], ("yb", d, i))
+        normalize(d)
+
+    def pass_eighths(tile, arrive, leave):
+        for i in range(3):
+            ref = tile.at[rows_at(from_y[i] * QR + (1 - par) * 16, 16)]
+            got(lambda: ref, (arrive, i))
+            put(lambda: (ref, ref, dev(x, y, zn, k)), (leave, i))
+
+    def take_eighths(tile, arrive):
+        got(lambda: tile.at[mine8], (arrive, 3))
+        for i in range(3):
+            got(lambda: tile.at[rows_at(from_y[i] * QR + par * 16, 16)], (arrive, i))
 
     def hid(t):
-        return lax.dot_general(w_in[...], X[t], NT, preferred_element_type=F32)
+        return lax.dot_general(w_in[...], N[t], NT, preferred_element_type=F32)
 
     def grad(t):
         return lax.dot_general(w_out[...], C[t], NT, preferred_element_type=F32)
@@ -284,20 +324,29 @@
     hs[0] = hid(tiles[1])
     put(lambda: (hs.at[0], hr.at[0], core), ("hc", 0))
     near = hid(tiles[0])
-    for i in range(3):
-        got(lambda: C.at[tiles[2], rows_at(from_y[i] * QR, QR)], ("cy", i))
-    put(lambda: (C.at[tiles[2]], C.at[tiles[2]], core), ("cf",))
+    pass_eighths(C.at[tiles[2]], "cy", "ce")
+    pass_eighths(X.at[tiles[3]], "ye", "ze")
     got(lambda: hr.at[0], ("hc", 0))
     h_near = near + hr[0]
     us[0] = h_near.astype(BF16)
     put(lambda: (us.at[0], ur.at[1], pair), ("hz", 0))
     hs[2] = h_near
+    take_eighths(C.at[tiles[2]], "ce")
+    put(lambda: (C.at[tiles[2]], C.at[tiles[2]], core), ("cf",))
     got(lambda: C.at[tiles[1]], ("cc",))
     got(lambda: C.at[tiles[3]], ("cf",))
     for i in (1, 0, 2):
         qs[i] = grad(xs[i]).astype(BF16)
         put(lambda: (qs.at[i], qr.at[i], dev(xs[i], y, z, k)), ("ga", i))
     own = grad(x)
+    for i in range(3):
+        got(lambda: X.at[tiles[2], rows_at(from_y[i] * QR, QR)], ("yq", i))
+    normalize(2)
+    far = hid(tiles[2])
+    take_eighths(X.at[tiles[3]], "ze")
+    normalize(3)
+    hs[1] = hid(tiles[3])
+    put(lambda: (hs.at[1], hr.at[1], core), ("hc", 1))
     for i in range(3):
         got(lambda: qr.at[i], ("ga", i))
     ts[...] = (own + qr[0].astype(F32) + qr[1].astype(F32) + qr[2].astype(F32)).astype(BF16)
@@ -311,12 +360,6 @@
     def _():
         tr[zh] = ts[...]
 
-    for d in (2, 3):
-        for i in range(3):
-            got(lambda: X.at[tiles[d], rows_at(from_y[i] * QR, QR)], ("yq", d, i))
-    hs[1] = hid(tiles[3])
-    put(lambda: (hs.at[1], hr.at[1], core), ("hc", 1))
-    far = hid(tiles[2])
     got(lambda: hr.at[1], ("hc", 1))
     h_far = far + hr[1]
     us[1] = h_far.astype(BF16)
@@ -330,99 +373,65 @@
         gA[k * 2 + half, x] = (tr[half].astype(F32) * slope).astype(BF16)
         at[half] = act.astype(BF16)
 
-    def spread_gh(step, pos):
-        ref = gA.at[pos, x]
+    def spread(step, half):
+        for i, p in enumerate(xs):
+            put(lambda: (at.at[half], aT.at[k * 2 + half], dev(p, y, z, k)), ("ax", 0, step), diag)
+        for i, p in enumerate(xs):
+            put(lambda: (at.at[half], aT.at[k * 2 + half], dev(p, y, z, 1 - k)),
+                ("ax", 1, step), beside)
+        put(lambda: (at.at[half], aT.at[k * 2 + half], core), ("ax", 1, step), beside)
+
+        @pl.when(diag)
+        def _():
+            aT[k * 2 + half] = at[half]
+
+        ref = gA.at[k * 2 + half, x]
         for i in (1, 0, 2):
             put(lambda: (ref, ref, dev(xs[i], y, z, k)), ("gg", step, i))
         put(lambda: (ref, ref, core), ("gc", step))
 
-    got(lambda: ur.at[1], ("hz", 0))
-    activate(1, 1 - zh)
-    spread_gh(1, k * 2 + 1 - zh)
-    got(lambda: ur.at[0], ("hz", 1))
-    activate(0, zh)
-    spread_gh(0, k * 2 + zh)
-    held = pl.ds(k * 2, 2)
-    for i, p in enumerate(xs):
-        put(lambda: (at, aT.at[held], dev(p, y, z, k)), ("ax", 0), diag)
-    for i, p in enumerate(xs):
-        put(lambda: (at, aT.at[held], dev(p, y, z, 1 - k)), ("ax", 1), beside)
-    put(lambda: (at, aT.at[held], core), ("ax", 1), beside)
-
-    @pl.when(diag)
-    def _():
-        aT[held] = at[...]
-
-    unheld = pl.ds((1 - k) * 2, 2)
-    for i in (0, 2, 1):
-        for step, pos in ((1, k * 2 + 1 - zh), (0, k * 2 + zh)):
-            got(lambda: gA.at[pos, from_x[i]], ("gg", step, i))
-        put(lambda: (gA.at[held, from_x[i]], gA.at[held, from_x[i]], core), ("gf", i))
-    for i in range(3):
-        got(lambda: WX.at[from_x[i]], ("wx", i))
-    got(lambda: gA.at[(1 - k) * 2 + 1 - zh, x], ("gc", 1))
-    got(lambda: gA.at[(1 - k) * 2 + zh, x], ("gc", 0))
-    for i in (0, 2, 1):
-        got(lambda: gA.at[unheld, from_x[i]], ("gf", i))
-
-    slab = WX[...].reshape(NX * HIDT, PC)
-    for p in range(4):
-        g0[p] = lax.dot_general(
-            gA[p].reshape(NX * HIDT, TOK), slab, TN, preferred_element_type=F32)
-    gq[...] = g0[...].astype(BF16)
-    for i in (1, 0, 2):
-        put(lambda: (gq.at[:, rows_at(ys[i] * QR, QR)], g1r.at[i], dev(x, ys[i], z, k)), ("gy", i))
-
-    got(lambda: aT.at[held], ("ax", 0), no(diag))
-    got(lambda: aT.at[unheld], ("ax", 1))
-    halves = (1 - zh, zh)
-
     def part_o(pos):
         return lax.dot_general(aT[pos], w_out[...], TN, preferred_element_type=F32)
 
-    for c in range(2):
-        os[c] = part_o((1 - k) * 2 + halves[c]).astype(BF16)
+    halves = (1 - zh, zh)
+
+    def outputs(c):
+        step, half = 1 - c, halves[c]
+        held, unheld = k * 2 + half, (1 - k) * 2 + half
+        got(lambda: aT.at[held], ("ax", 0, step), no(diag))
+        got(lambda: aT.at[unheld], ("ax", 1, step))
+        os[c] = part_o(unheld).astype(BF16)
         put(lambda: (os.at[c], orr.at[c], core), ("oc", c))
-    for c in range(2):
-        o0[c] = part_o(k * 2 + halves[c])
-    for c in range(2):
+        o0[c] = part_o(held)
+        for i in (0, 2, 1):
+            ref = gA.at[held, from_x[i]]
+            got(lambda: ref, ("gg", step, i))
+            put(lambda: (ref, ref, core), ("gf", step, i))
         got(lambda: orr.at[c], ("oc", c))
         o1[c] = (o0[c] + orr[c].astype(F32)).astype(BF16)
         for i in (1, 0, 2):
             put(lambda: (o1.at[c, :, cols(ys[i])], o1r.at[c, i], dev(x, ys[i], z, k)), ("oy", c, i))
-
-    def weight_grad(left, right):
-        acc = jnp.dot(left(0), right[0], preferred_element_type=F32)
-        for t in range(1, 4):
-            acc = acc + jnp.dot(left((t % 2) * 2 + t // 2), right[t], preferred_element_type=F32)
-        return acc.astype(BF16)
-
-    g_out[...] = weight_grad(lambda p: aT[p], C)
-    stores = [pltpu.make_async_copy(g_out, gout_any, lsem.at[6])]
-    stores[0].start()
-
-    for i in range(3):
-        got(lambda: g1r.at[i], ("gy", i))
-    g2[...] = (
-        g0[:, quarter, :] + g1r[0].astype(F32) + g1r[1].astype(F32) + g1r[2].astype(F32)
-    ).astype(BF16)
+    def features(c):
+        step, half = 1 - c, halves[c]
+        unheld = (1 - k) * 2 + half
+        if c == 0:
+            for i in range(3):
+                got(lambda: WX.at[from_x[i]], ("wx", i))
+        got(lambda: gA.at[unheld, x], ("gc", step))
+        for i in (0, 2, 1):
+            got(lambda: gA.at[unheld, from_x[i]], ("gf", step, i))
+        slab = WX[...].reshape(NX * HIDT, PC)
+        for j in range(2):
+            g0[c, j] = lax.dot_general(
+                gA[j * 2 + half].reshape(NX * HIDT, TOK), slab, TN, preferred_element_type=F32)
+        gq[c] = g0[c].astype(BF16)
+        for i in (1, 0, 2):
+            put(lambda: (gq.at[c, :, rows_at(ys[i] * QR, QR)], g1r.at[c, i],
+                         dev(x, ys[i], z, k)), ("gy", c, i))
+
     zsem = w.block("gz", NL)
-    for p in range(4):
-        for e in range(2):
-            target = (p % 2) * NL + zh * 4 + (p // 2) * 2 + e
-            put(lambda: (g2.at[p, pl.ds(e * 16, 16)], g2r.at[zl], dev(x, y, target, k)),
-                zsem(zl), z != target)
-    mine_here = zr == zh
-
-    @pl.when(mine_here)
-    def _():
-        g2r[zl] = g2[kt * 2 + zh, rows_at(ze * 16, 16), :]
-
-    g_in[...] = weight_grad(lambda p: gA[p, x], X)
-    stores.append(pltpu.make_async_copy(g_in, gin_any, lsem.at[7]))
-    stores[1].start()
-
-    for c in range(2):
+
+    def sums_y(c):
         for i in range(3):
             got(lambda: o1r.at[c, i], ("oy", c, i))
         o2[c] = (
@@ -432,6 +441,52 @@
         for d in range(c, NL):
             target = halves[c] * NL + ls[d]
             put(lambda: (o2.at[c, prow(ls[d])], o2r.at[c, d], dev(x, y, target, k)), ("oz", c, d))
+
+    def feature_sums(c):
+        for i in range(3):
+            got(lambda: g1r.at[c, i], ("gy", c, i))
+        g2[c] = (
+            g0[c, :, quarter, :] + g1r[c, 0].astype(F32)
+            + g1r[c, 1].astype(F32) + g1r[c, 2].astype(F32)
+        ).astype(BF16)
+        for j in range(2):
+            for e in range(2):
+                target = halves[c] * NL + zh * 4 + j * 2 + e
+                put(lambda: (g2.at[c, j, pl.ds(e * 16, 16)], g2r.at[zl], dev(x, y, target, k)),
+                    zsem(zl), (z != target) if c else None)
+
+    got(lambda: ur.at[1], ("hz", 0))
+    activate(1, 1 - zh)
+    spread(1, 1 - zh)
+    got(lambda: ur.at[0], ("hz", 1))
+    activate(0, zh)
+    spread(0, zh)
+    outputs(0)
+    outputs(1)
+    features(0)
+    features(1)
+    sums_y(0)
+    sums_y(1)
+    feature_sums(0)
+
+    def weight_grad(left, right):
+        wide = jnp.concatenate([left((t % 2) * 2 + t // 2) for t in range(4)], axis=1)
+        tall = right[...].reshape(4 * TOK, FEAT)
+        return jnp.dot(wide, tall, preferred_element_type=F32).astype(BF16)
+
+    g_out[...] = weight_grad(lambda p: aT[p], C)
+    stores = [pltpu.make_async_copy(g_out, gout_any, lsem.at[6])]
+    stores[0].start()
+    feature_sums(1)
+    mine_here = zr == zh
+
+    @pl.when(mine_here)
+    def _():
+        g2r[zl] = g2[1, kt, rows_at(ze * 16, 16), :]
+
+    g_in[...] = weight_grad(lambda p: gA[p, x], N)
+    stores.append(pltpu.make_async_copy(g_in, gin_any, lsem.at[7]))
+    stores[1].start()
 
     for n in range(NL):
         got(lambda: g2r.at[n], zsem(n), no(both(mine_here, zl == n)))
@@ -509,6 +564,17 @@
     assert len(w.sent) <= N_SEND and len(w.slots) <= N_RECV
 
 
+def hand_kernel(a, b, c, d, ao, bo, co, do, sem):
+    copies = [
+        pltpu.make_async_copy(src, dst, sem.at[i])
+        for i, (src, dst) in enumerate(((a, ao), (b, bo), (c, co), (d, do)))
+    ]
+    for copy in copies:
+        copy.start()
+    for copy in copies:
+        copy.wait()
+
+
 def per_device(inputs, cotangent, ln_gain, ln_bias, w_in, w_out):
     dma = pltpu.SemaphoreType.DMA
     tile = jax.ShapeDtypeStruct((TOK, FEAT), BF16)
@@ -520,7 +586,7 @@
     def vf(*shape):
         return pltpu.VMEM(shape, F32)
 
-    out, gx, g_in, g_out = pl.pallas_call(
+    results = pl.pallas_call(
         layer_kernel,
         name="layer",
         out_shape=[tile, tile, grad, grad],
@@ -528,12 +594,13 @@
         out_specs=[HBM] * 4,
         scratch_shapes=[
             vb(TOK, FEAT), vb(TOK, FEAT), vf(FEAT), vf(FEAT), vb(HIDT, FEAT), vb(HIDT, FEAT),
-            vb(4, TOK, FEAT), vb(4, TOK, FEAT), vb(TOK, FEAT), vf(4, 8, TOK), vf(TOK, TOK),
+            vb(4, TOK, FEAT), vb(4, TOK, FEAT), vb(4, TOK, FEAT), vf(4, 8, TOK), vf(4, 8, TOK),
+            vf(2, FEAT), vf(TOK, TOK),
             vf(4, HIDT, TOK), vf(2, HIDT, TOK), vb(2, HIDT, TOK), vb(2, HIDT, TOK),
             vb(3, HIDT, TOK), vb(3, HIDT, TOK), vb(HIDT, TOK), vb(2, HIDT, TOK),
             vb(4, HIDT, TOK), vb(2, HIDT, TOK),
-            vb(NX, HIDT, PC), vb(4, NX, HIDT, TOK), vf(4, TOK, PC), vb(4, TOK, PC), vb(3, 4, QR, PC),
-            vb(4, QR, PC), vb(NL, PR, PC), vb(PR, PC), vb(TOK, FEAT), vf(TOK, FEAT), vf(TOK, TOK),
+            vb(NX, HIDT, PC), vb(4, NX, HIDT, TOK), vf(2, 2, TOK, PC), vb(2, 2, TOK, PC), vb(2, 3, 2, QR, PC),
+            vb(2, 2, QR, PC), vb(NL, PR, PC), vb(PR, PC), vb(TOK, FEAT), vf(TOK, FEAT), vf(TOK, TOK),
             vb(2, TOK, FEAT), vb(2, TOK, FEAT), vf(2, TOK, FEAT), vb(2, TOK, FEAT),
             vb(2, 3, TOK, PC), vb(2, TOK, PC), vb(2, NL, PR, PC), vf(16, 8, TOK),
             vb(TOK, FEAT), vb(TOK, FEAT), vb(HIDT, FEAT), vb(HIDT, FEAT),
@@ -543,6 +610,14 @@
             collective_id=0, has_side_effects=True, vmem_limit_bytes=63 << 20
         ),
     )(inputs, cotangent, ln_gain, ln_bias, w_in.T, w_out)
+    out, gx, g_in, g_out = pl.pallas_call(
+        hand_kernel,
+        name="hand",
+        out_shape=[tile, tile, grad, grad],
+        in_specs=[VMEM] * 4,
+        out_specs=[HBM] * 4,
+        scratch_shapes=[dma((4,))],
+    )(*results)
     return out, gx, g_in.T, g_out
 
 

time: 116 us -> 112 us (0.966)
  the two profiles are of different devices: /device:TPU:6 before, /device:TPU:1 now
where the time goes in v4:
time: 112 us
  Pallas kernels  111 us (99%)
    pallas_call x1, Pallas kernels, per_device(): pl.pallas_call(layer_kernel, name='layer', out_shape=[tile, tile, grad, g...  108 us
    pallas_call x1, Pallas kernels, per_device(): pl.pallas_call(hand_kernel, name='hand', out_shape=[tile, tile, grad, gra...  2.78 us

profile of v4, /device:TPU:1, one launch (start us, length us, event | category | flops | bytes accessed | tf_op | source)
XLA Modules:
  0.0 111.8 jit_solution(9153215562224475179)
XLA Ops:
  0.6 108.4 %layer.1 = (bf16[128,1536]{1,0:T(8,128)(2,1)}, bf16[128,1536]{1,0:T(8,128)(2,1)}, bf16[192,1536]{1,0:T(8,128)(2,1)}, bf16[192,1536]{1,0:T(8,128)(2,1)}) custom-call(bf16[128,1536]{1,0:T(8,128)(2,1)} %x_any.1, bf16[128,1536]{1,0:T(8,128)(2,1)} %cot_any.1, f32[1536]{0:T(1024)} %gain_any.1, f32[1536]{0:T(1024)} %bias_any.1, bf16[192,1536]{1,0:T(8,128)(2,1)} %bitcast.2, ...), custom_call_target="tpu_custom_call" | custom-call | tf_op jit(solution)/shard_map/layer/pallas_call | solution.py:589
  109.0 2.8 %hand.1 = (bf16[128,1536]{1,0:T(8,128)(2,1)}, bf16[128,1536]{1,0:T(8,128)(2,1)}, bf16[192,1536]{1,0:T(8,128)(2,1)}, bf16[192,1536]{1,0:T(8,128)(2,1)}) custom-call(bf16[128,1536]{1,0:T(8,128)(2,1)} %get-tuple-element.12.a, bf16[128,1536]{1,0:T(8,128)(2,1)} %get-tuple-element.13.b, bf16[192,1536]{1,0:T(8,128)(2,1)} %get-tuple-element.14.c, ...), custom_call_target="tpu_custom_call" | custom-call | tf_op jit(solution)/shard_map/hand/pallas_call | solution.py:613

commit v5 on v4

--- a/solution.py
+++ b/solution.py
@@ -122,14 +122,14 @@
     hs, hr, us, ur, qs, qr, ts, tr, aT, at,
     WX, gA, g0, gq, g1r, g2, g2r, gp, gn, sc, stb,
     os, orr, o0, o1, o1r, o2, o2r, stats, out, gx, g_in, g_out,
-    ssem, rsem, lsem,
+    ssem, rsem, dsem,
 ):
     x, y, z, zh, zl, k, r = place()
     no = jnp.logical_not
     w = Wires(ssem, rsem)
     put, got = w.put, w.got
     loads = [
-        pltpu.make_async_copy(src, dst, lsem.at[i])
+        pltpu.make_async_copy(src, dst, dsem.at[i])
         for i, (src, dst) in enumerate((
             (x_any, x_ref), (cot_any, cot_ref), (gain_any, gain_ref),
             (bias_any, bias_ref), (win_any, w_in), (wout_any, w_out),
@@ -158,8 +158,8 @@
         when(pred, lambda: pl.semaphore_signal(
             barrier, inc=1, device_id=peer, device_id_type=pl.DeviceIdType.MESH))
 
-    for p in zs:
-        greet(dev(x, y, p, k))
+    for d in (8, 7, 9, 6, 10, 5, 11, 4, 12, 3, 13, 2, 14, 1, 15):
+        greet(dev(x, y, zs[d - 1], k))
     greet(core)
     greet(dev(x, y, zm, 1 - k))
     for dx in range(4):
@@ -475,7 +475,7 @@
         return jnp.dot(wide, tall, preferred_element_type=F32).astype(BF16)
 
     g_out[...] = weight_grad(lambda p: aT[p], C)
-    stores = [pltpu.make_async_copy(g_out, gout_any, lsem.at[6])]
+    stores = [pltpu.make_async_copy(g_out, gout_any, dsem.at[6])]
     stores[0].start()
     feature_sums(1)
     mine_here = zr == zh
@@ -485,7 +485,7 @@
         g2r[zl] = g2[1, kt, rows_at(ze * 16, 16), :]
 
     g_in[...] = weight_grad(lambda p: gA[p, x], N)
-    stores.append(pltpu.make_async_copy(g_in, gin_any, lsem.at[7]))
+    stores.append(pltpu.make_async_copy(g_in, gin_any, dsem.at[7]))
     stores[1].start()
 
     for n in range(NL):
@@ -513,12 +513,28 @@
         for d in range(c, NL):
             piece = piece + o2r[c, d].astype(F32)
     out[mine] = (x_ref[mine].astype(F32) + piece).astype(BF16)
-    for d in range(1, NL):
-        put(lambda: (out.at[mine], out.at[mine], dev(x, y, zh * NL + ls[d], k)), ("oal", d))
+    lsem = w.block("oal", NL)
+    for d in (4, 3, 5, 2, 6, 1, 7):
+        put(lambda: (out.at[mine], out.at[mine], dev(x, y, zh * NL + ls[d], k)), lsem(zl))
 
     mean, rstd = st_ref[:, 0:1], st_ref[:, 1:2]
     sc[...] = (x_ref[...].astype(F32) - mean) * rstd
     stb[...] = jnp.zeros((TOK, TOK), F32)
+    group = lax.div(zl, 4)
+    groups = (group, 1 - group)
+
+    def strip(n, q):
+        return out.at[(rows_at(groups[n] * 64, 64), cols(q))]
+
+    def send_strip(n):
+        for i in range(4):
+            source = groups[n] * 4 + i
+            got(lambda: out.at[prow(source), cols(y)], lsem(source),
+                (zl != source) if n == 0 else None)
+        for i in (1, 0, 2):
+            put(lambda: (strip(n, y), strip(n, y), dev(x, ys[i], z, k)), ("oay", n, i))
+
+    send_strip(0)
     for q in range(NX):
         for e in range(2):
             got(lambda: gn.at[rows_at(y * QR + e * 16, 16), pl.ds(q * PC, PC)], asem(q * 2 + e),
@@ -536,11 +552,7 @@
             if dx or dy:
                 put(lambda: (stats.at[0], stats.at[dx * 4 + dy],
                              dev(lax.rem(x + dx, NX), lax.rem(y + dy, NY), z, k)), ("ls", dx, dy))
-    from_l = [lax.rem(zl + NL - d, NL) for d in range(NL)]
-    for d in range(1, NL):
-        got(lambda: out.at[prow(from_l[d]), cols(y)], ("oal", d))
-    for i in (1, 0, 2):
-        put(lambda: (out.at[:, cols(y)], out.at[:, cols(y)], dev(x, ys[i], z, k)), ("oay", i))
+    send_strip(1)
     for n in range(1, 16):
         got(lambda: stats.at[n], ("ls", n // 4, n % 4))
     sums_all = stats[0]
@@ -552,11 +564,12 @@
     gz = gn[...].astype(F32) * gain
     delta = rstd * (gz - first / D - sc[...] * (second / D))
     gx[...] = (cot_ref[...].astype(F32) + delta).astype(BF16)
-    stores.append(pltpu.make_async_copy(gx, gx_any, lsem.at[9]))
+    stores.append(pltpu.make_async_copy(gx, gx_any, dsem.at[9]))
     stores[2].start()
-    for i in range(3):
-        got(lambda: out.at[:, cols(from_y[i])], ("oay", i))
-    stores.append(pltpu.make_async_copy(out, out_any, lsem.at[8]))
+    for n in range(2):
+        for i in range(3):
+            got(lambda: strip(n, from_y[i]), ("oay", n, i))
+    stores.append(pltpu.make_async_copy(out, out_any, dsem.at[8]))
     stores[3].start()
     w.finish()
     for store in stores:

time: 112 us -> 111 us (level)
  the two profiles are of different devices: /device:TPU:1 before, /device:TPU:6 now
where the time goes in v5:
time: 111 us
  Pallas kernels  110 us (99%)
    pallas_call x1, Pallas kernels, per_device(): pl.pallas_call(layer_kernel, name='layer', out_shape=[tile, tile, grad, g...  107 us
    pallas_call x1, Pallas kernels, per_device(): pl.pallas_call(hand_kernel, name='hand', out_shape=[tile, tile, grad, gra...  2.78 us

profile of v5, /device:TPU:6, one launch (start us, length us, event | category | flops | bytes accessed | tf_op | source)
XLA Modules:
  0.0 110.9 jit_solution(942468161776810458)
XLA Ops:
  0.6 107.5 %layer.1 = (bf16[128,1536]{1,0:T(8,128)(2,1)}, bf16[128,1536]{1,0:T(8,128)(2,1)}, bf16[192,1536]{1,0:T(8,128)(2,1)}, bf16[192,1536]{1,0:T(8,128)(2,1)}) custom-call(bf16[128,1536]{1,0:T(8,128)(2,1)} %x_any.1, bf16[128,1536]{1,0:T(8,128)(2,1)} %cot_any.1, f32[1536]{0:T(1024)} %gain_any.1, f32[1536]{0:T(1024)} %bias_any.1, bf16[192,1536]{1,0:T(8,128)(2,1)} %bitcast.2, ...), custom_call_target="tpu_custom_call" | custom-call | tf_op jit(solution)/shard_map/layer/pallas_call | solution.py:602
  108.1 2.8 %hand.1 = (bf16[128,1536]{1,0:T(8,128)(2,1)}, bf16[128,1536]{1,0:T(8,128)(2,1)}, bf16[192,1536]{1,0:T(8,128)(2,1)}, bf16[192,1536]{1,0:T(8,128)(2,1)}) custom-call(bf16[128,1536]{1,0:T(8,128)(2,1)} %get-tuple-element.12.a, bf16[128,1536]{1,0:T(8,128)(2,1)} %get-tuple-element.13.b, bf16[192,1536]{1,0:T(8,128)(2,1)} %get-tuple-element.14.c, ...), custom_call_target="tpu_custom_call" | custom-call | tf_op jit(solution)/shard_map/hand/pallas_call | solution.py:626

commit v6 on v5

--- a/solution.py
+++ b/solution.py
@@ -284,9 +284,6 @@
     got(lambda: X.at[tiles[2], quarter], ("xq",), no(diag))
     along_y(X.at[tiles[2], quarter], ("yq",))
     loads[4].wait()
-    for i in (1, 0, 2):
-        put(lambda: (w_in.at[:, cols(xs[i])], WX.at[x], dev(xs[i], y, z, k)), ("wx", i))
-    WX[x] = w_in[:, cols(x)]
     got(lambda: gb, ("gb",), no(diag))
 
     def normalize(d):
@@ -339,6 +336,9 @@
         qs[i] = grad(xs[i]).astype(BF16)
         put(lambda: (qs.at[i], qr.at[i], dev(xs[i], y, z, k)), ("ga", i))
     own = grad(x)
+    for i in (1, 0, 2):
+        put(lambda: (w_in.at[:, cols(xs[i])], WX.at[x], dev(xs[i], y, z, k)), ("wx", i))
+    WX[x] = w_in[:, cols(x)]
     for i in range(3):
         got(lambda: X.at[tiles[2], rows_at(from_y[i] * QR, QR)], ("yq", i))
     normalize(2)

time: 111 us -> 112 us (level)
  no operation moved by 1% of the time
where the time goes in v6:
time: 112 us; the launch traced here: 111 us
  Pallas kernels  111 us (99%)
    pallas_call x1, Pallas kernels, per_device(): pl.pallas_call(layer_kernel, name='layer', out_shape=[tile, tile, grad, g...  108 us
    pallas_call x1, Pallas kernels, per_device(): pl.pallas_call(hand_kernel, name='hand', out_shape=[tile, tile, grad, gra...  2.78 us

profile of v6, /device:TPU:6, one launch (start us, length us, event | category | flops | bytes accessed | tf_op | source)
XLA Modules:
  0.0 111.4 jit_solution(13249287870291492164)
XLA Ops:
  0.6 108.0 %layer.1 = (bf16[128,1536]{1,0:T(8,128)(2,1)}, bf16[128,1536]{1,0:T(8,128)(2,1)}, bf16[192,1536]{1,0:T(8,128)(2,1)}, bf16[192,1536]{1,0:T(8,128)(2,1)}) custom-call(bf16[128,1536]{1,0:T(8,128)(2,1)} %x_any.1, bf16[128,1536]{1,0:T(8,128)(2,1)} %cot_any.1, f32[1536]{0:T(1024)} %gain_any.1, f32[1536]{0:T(1024)} %bias_any.1, bf16[192,1536]{1,0:T(8,128)(2,1)} %bitcast.2, ...), custom_call_target="tpu_custom_call" | custom-call | tf_op jit(solution)/shard_map/layer/pallas_call | solution.py:602
  108.6 2.8 %hand.1 = (bf16[128,1536]{1,0:T(8,128)(2,1)}, bf16[128,1536]{1,0:T(8,128)(2,1)}, bf16[192,1536]{1,0:T(8,128)(2,1)}, bf16[192,1536]{1,0:T(8,128)(2,1)}) custom-call(bf16[128,1536]{1,0:T(8,128)(2,1)} %get-tuple-element.12.a, bf16[128,1536]{1,0:T(8,128)(2,1)} %get-tuple-element.13.b, bf16[192,1536]{1,0:T(8,128)(2,1)} %get-tuple-element.14.c, ...), custom_call_target="tpu_custom_call" | custom-call | tf_op jit(solution)/shard_map/hand/pallas_call | solution.py:626
